TPU v7x, 768 devices: a whole 4x8x12 slice. The times are simulated.
768 devices in a mesh: dom: 96 (over z, y), sub: 8 (over x, core).
Axes of the slice: x: 4, y: 8, z: 12, core: 2. Of those that a mesh axis runs over, the one named last changes fastest.
Arguments:
- state: float32 [128, 786432], P(None, ('dom', 'sub')), may hold values from -6 to 6
- cotangent: float32 [128, 786432], P(None, ('dom', 'sub')), may hold values from -6 to 6
- velocity: float32 [3, 786432], P(None, ('dom', 'sub')), may hold values from -4 to 4
- dispersion: float32 [786432], P(('dom', 'sub')), may hold values from 0.1 to 1
- retained: float32 [128, 786432], P(None, ('dom', 'sub')), may hold values from 0 to 0.9
- kappa: float32 [12288], P(('dom', 'sub')), may hold values from 1 to 40
- elem_block: int32 [786432], P(('dom', 'sub')), may hold values from 0 to 127
- face_source: int32 [6, 786432], P(None, ('dom', 'sub')), may hold values from 0 to 8448, as said below
- send_face: int32 [6, 294912], P(None, ('dom', 'sub')), may hold values from 0 to 6144, as said below
Outputs:
- advanced: float32 [128, 786432], P(None, ('dom', 'sub'))
- adjoint: float32 [128, 786432], P(None, ('dom', 'sub'))
- rate_grad: float32 [12288], P(('dom', 'sub'))
Inputs may be any that keep to these rules, and one draw needn't show every extreme that they name: `face_source`: own faces are numbered f * 1024 + e within a partition. Each own face names another own face that names it back, a slot 6144 + r * 384 + k of a used slot k of round r whose send_face entry is that very face, or the last value (outer boundary of the reach); no value but the last is named twice within a partition. `send_face`: in round r a partition lists its faces shared with the partition at dom offset o_r (same sub index) in the leading slots, the others hold 6144; slot k of round r at dom index d and slot k of round 2 * 3 - 1 - r at dom index d + o_r are the same face, and both partitions use equally many slots there. No round uses more than 384 slots, and some round of some partition uses all 384. Rounds leading outside the reach use none.
All inputs are finite; a program needn't handle non-finite values.
Results may differ from a plain program's by a relative error of at most 0.0001.
Values sent between devices are 32-bit elements; how exact they have to be, the bound alone decides.
A program may use at most 32 MiB of HBM per device.

v0:
```python
import jax
import jax.numpy as jnp
import numpy as np
from jax import lax
from jax.sharding import PartitionSpec as P

REACH = 3


STEP = 0.02
SECOND_SPECIES = 0.35


def shifted(block, axis, distance):
    devices = range(lax.axis_size(axis))
    route = [(i - distance, i) for i in devices if i - distance in devices]
    return lax.ppermute(block, axis, route)


def nodal_operator():
    inner_point = 1.0 / np.sqrt(5.0)
    points = np.array([-1.0, -inner_point, inner_point, 1.0])
    bary_weight = np.array(
        [1.0 / np.prod([points[j] - points[m] for m in range(4) if m != j]) for j in range(4)]
    )
    derivative = np.zeros((4, 4))
    for i in range(4):
        for j in range(4):
            if i != j:
                derivative[i, j] = bary_weight[j] / bary_weight[i] / (points[i] - points[j])
        derivative[i, i] = -np.sum(derivative[i])
    identity = np.eye(4)
    along_i = np.kron(identity, np.kron(identity, derivative))
    along_j = np.kron(identity, np.kron(derivative, identity))
    along_k = np.kron(derivative, np.eye(16))
    second = along_i @ along_i + along_j @ along_j + along_k @ along_k
    stacked = np.concatenate(
        [np.kron(np.eye(2), matrix) for matrix in (along_i, along_j, along_k, second)], axis=0
    )
    return jnp.asarray(stacked, dtype=jnp.float32)


def partner_offsets():
    return [number - REACH for number in range(REACH)] + [number + 1 for number in range(REACH)]


def face_traces(field):
    elem_count = field.shape[-1]
    node_cube = field.reshape(2, 4, 4, 4, elem_count)
    pieces = [
        node_cube[:, :, :, 0],
        node_cube[:, :, :, 3],
        node_cube[:, :, 0],
        node_cube[:, :, 3],
        node_cube[:, 0],
        node_cube[:, 3],
    ]
    return [piece.reshape(32, elem_count) for piece in pieces]


def add_to_faces(field, face_terms):
    elem_count = field.shape[-1]
    node_cube = field.reshape(2, 4, 4, 4, elem_count)
    shaped = [face_term.reshape(2, 4, 4, elem_count) for face_term in face_terms]
    node_cube = node_cube.at[:, :, :, 0].add(shaped[0])
    node_cube = node_cube.at[:, :, :, 3].add(shaped[1])
    node_cube = node_cube.at[:, :, 0].add(shaped[2])
    node_cube = node_cube.at[:, :, 3].add(shaped[3])
    node_cube = node_cube.at[:, 0].add(shaped[4])
    node_cube = node_cube.at[:, 3].add(shaped[5])
    return node_cube.reshape(128, elem_count)


def face_weights(velocity):
    weights = []
    for face_number in range(6):
        normal_sign = 1.0 if face_number % 2 == 1 else -1.0
        weights.append(6.0 * jnp.minimum(normal_sign * velocity[face_number // 2], 0.0))
    return weights


def volume_flow(operator, field, velocity, dispersion):
    images = jnp.dot(
        operator, field, precision=lax.Precision.HIGHEST, preferred_element_type=jnp.float32
    )
    return (
        -velocity[0] * images[0:128]
        - velocity[1] * images[128:256]
        - velocity[2] * images[256:384]
        + dispersion * images[384:512]
    )


def volume_adjoint(operator, field, velocity, dispersion):
    scaled = jnp.concatenate(
        [-velocity[0] * field, -velocity[1] * field, -velocity[2] * field, dispersion * field],
        axis=0,
    )
    return jnp.dot(
        operator.T, scaled, precision=lax.Precision.HIGHEST, preferred_element_type=jnp.float32
    )


def outgoing(state, cotangent, velocity, send_face):
    weights = face_weights(velocity)
    state_traces = face_traces(state)
    cotangent_traces = face_traces(cotangent)
    pulled = jnp.concatenate(
        [weights[face_number] * cotangent_traces[face_number] for face_number in range(6)], axis=1
    )
    own_both = jnp.concatenate([jnp.concatenate(state_traces, axis=1), -pulled], axis=0)
    own_table = jnp.concatenate([own_both, jnp.zeros((64, 1), jnp.float32)], axis=1)
    send_both = own_table[:, send_face]
    return (send_both, (state_traces, cotangent_traces, weights, own_both))


def finish(
    operator,
    state,
    cotangent,
    velocity,
    dispersion,
    retained,
    elem_rate,
    face_source,
    local_parts,
    arrived_both,
):
    state_traces, cotangent_traces, weights, own_both = local_parts
    elem_count = state.shape[1]
    species_gain = jnp.where(jnp.arange(128) < 64, 1.0, SECOND_SPECIES).astype(jnp.float32)
    uptake = elem_rate[None, :] * species_gain[:, None] * (1.0 - retained)
    full_table = jnp.concatenate(
        [own_both, arrived_both.reshape(64, -1), jnp.zeros((64, 1), jnp.float32)], axis=1
    )
    picked = full_table[:, face_source.reshape(-1)]
    outer = picked[:32]
    back = picked[32:]
    state_terms = [
        weights[face_number]
        * (
            state_traces[face_number]
            - outer[:, face_number * elem_count : (face_number + 1) * elem_count]
        )
        for face_number in range(6)
    ]
    advanced = state + STEP * add_to_faces(
        volume_flow(operator, state, velocity, dispersion) - uptake * state, state_terms
    )
    cotangent_terms = [
        weights[face_number] * cotangent_traces[face_number]
        + back[:, face_number * elem_count : (face_number + 1) * elem_count]
        for face_number in range(6)
    ]
    adjoint = cotangent + STEP * add_to_faces(
        volume_adjoint(operator, cotangent, velocity, dispersion) - uptake * cotangent,
        cotangent_terms,
    )
    elem_terms = jnp.sum(cotangent * species_gain[:, None] * (1.0 - retained) * state, axis=0)
    return (advanced, adjoint, elem_terms)


def shards(
    state, cotangent, velocity, dispersion, retained, kappa, elem_block, face_source, send_face
):
    rounds = send_face.shape[0]
    offsets = partner_offsets()
    operator = nodal_operator()
    row_rates = lax.all_gather(kappa, "sub", axis=0, tiled=True)
    block_hits = (
        jnp.arange(row_rates.shape[0], dtype=jnp.int32)[:, None] == elem_block[None, :]
    ).astype(jnp.float32)
    elem_rate = jnp.sum(block_hits * row_rates[:, None], axis=0)
    send_both, local_parts = outgoing(state, cotangent, velocity, send_face)
    arrived = [None] * rounds
    for round_number in range(rounds):
        source_round = rounds - 1 - round_number
        arrived[round_number] = shifted(send_both[:, source_round], "dom", -offsets[round_number])
    arrived_both = jnp.stack(arrived, axis=1)
    advanced, adjoint, elem_terms = finish(
        operator,
        state,
        cotangent,
        velocity,
        dispersion,
        retained,
        elem_rate,
        face_source,
        local_parts,
        arrived_both,
    )
    owned = lax.psum_scatter(
        jnp.sum(block_hits * elem_terms[None, :], axis=1), "sub", scatter_dimension=0, tiled=True
    )
    rate_grad = -STEP * owned
    return (advanced, adjoint, rate_grad)


def solution(mesh):
    return jax.shard_map(
        shards,
        mesh=mesh,
        in_specs=(
            P(None, ("dom", "sub")),
            P(None, ("dom", "sub")),
            P(None, ("dom", "sub")),
            P(("dom", "sub")),
            P(None, ("dom", "sub")),
            P(("dom", "sub")),
            P(("dom", "sub")),
            P(None, ("dom", "sub")),
            P(None, ("dom", "sub")),
        ),
        out_specs=(P(None, ("dom", "sub")), P(None, ("dom", "sub")), P(("dom", "sub"))),
        check_vma=False,
    )
```

profile of v0, /device:TPU:521, one launch (start us, length us, event | category | flops | bytes accessed | tf_op | source)
XLA Modules:
  0.0 143.7 jit_solution(324710414240084857)
XLA Ops:
  0.6 1.2 reshape.556
  1.9 0.7 slice_reduce_fusion
  2.9 0.7 slice_reduce_fusion.2
  3.7 0.6 slice_negate_fusion.1
  4.8 0.2 copy-done.10
  5.6 0.6 copy-done.22
  6.5 0.4 copy-done.25
  7.2 2.3 %copy.338 = f32[64,6144]{0,1:T(8,128)} copy(f32[64,6144]{1,0:T(8,128)S(1)} %pad_maximum_fusion) | data formatting | bytes 3145728
  9.5 2.1 %concatenate.45.clone = f32[64,6145]{0,1:T(8,128)S(1)} pad(f32[64,6144]{0,1:T(8,128)} %copy.338, f32[]{:T(128)} %constant.294.clone.1), padding=0_0x0_1 | pad | bytes 3145988 | tf_op jit(solution)/shard_map/concatenate | solution.py:112
  11.6 5.1 %gather_fusion = f32[2304,64]{1,0:T(8,128)} fusion(f32[64,6145]{0,1:T(8,128)S(1)} %concatenate.45.clone, s32[3072]{0:T(1024)S(1)} %pad_clamp_fusion), kind=kCustom, calls=%fused_computation | custom fusion | bytes 1188864 | tf_op jit(solution)/shard_map/gather | solution.py:113
  16.7 1.7 %copy.305 = f32[6,384,64]{1,2,0:T(8,128)S(1)} copy(f32[6,384,64]{2,1,0:T(8,128)} %bitcast.85) | data formatting | bytes 1179648 | tf_op jit(solution)/shard_map/gather | solution.py:113
  18.5 6.6 %collective-permute-start = (f32[64,384]{1,0:T(8,128)S(1)}, f32[64,384]{1,0:T(8,128)}, u32[]{:S(2)}, u32[]{:S(2)}) collective-permute-start(f32[64,384]{1,0:T(8,128)S(1)} %get-tuple-element.178), channel_id=1, source_target_pairs={{0,24},{8,32},{16,40},{24,48},{32,56},{40,64},{48,72},{56,80},{64,... | collective-permute-start | bytes 294920 | tf_op jit(solution)/shard_map/ppermute | solution.py:17
  25.1 2.4 %collective-permute-start.1 = (f32[64,384]{1,0:T(8,128)S(1)}, f32[64,384]{1,0:T(8,128)}, u32[]{:S(2)}, u32[]{:S(2)}) collective-permute-start(f32[64,384]{1,0:T(8,128)S(1)} %get-tuple-element.177), channel_id=1, source_target_pairs={{0,16},{8,24},{16,32},{24,40},{32,48},{40,56},{48,64},{56,72},{64,... | collective-permute-start | bytes 294920 | tf_op jit(solution)/shard_map/ppermute | solution.py:17
  27.5 2.3 %collective-permute-start.2 = (f32[64,384]{1,0:T(8,128)S(1)}, f32[64,384]{1,0:T(8,128)}, u32[]{:S(2)}, u32[]{:S(2)}) collective-permute-start(f32[64,384]{1,0:T(8,128)S(1)} %get-tuple-element.176), channel_id=1, source_target_pairs={{0,8},{8,16},{16,24},{24,32},{32,40},{40,48},{48,56},{56,64},{64,7... | collective-permute-start | bytes 294920 | tf_op jit(solution)/shard_map/ppermute | solution.py:17
  29.8 3.0 %collective-permute-start.3 = (f32[64,384]{1,0:T(8,128)S(1)}, f32[64,384]{1,0:T(8,128)}, u32[]{:S(2)}, u32[]{:S(2)}) collective-permute-start(f32[64,384]{1,0:T(8,128)S(1)} %get-tuple-element.175), channel_id=1, source_target_pairs={{8,0},{16,8},{24,16},{32,24},{40,32},{48,40},{56,48},{64,56},{72,6... | collective-permute-start | bytes 294920 | tf_op jit(solution)/shard_map/ppermute | solution.py:17
  32.8 7.1 %collective-permute-start.4 = (f32[64,384]{1,0:T(8,128)S(1)}, f32[64,384]{1,0:T(8,128)}, u32[]{:S(2)}, u32[]{:S(2)}) collective-permute-start(f32[64,384]{1,0:T(8,128)S(1)} %get-tuple-element.174), channel_id=1, source_target_pairs={{16,0},{24,8},{32,16},{40,24},{48,32},{56,40},{64,48},{72,56},{80,... | collective-permute-start | bytes 294920 | tf_op jit(solution)/shard_map/ppermute | solution.py:17
  40.0 1.4 fusion.29
  42.2 0.2 dynamic-update-slice.36
  42.4 13.8 %all-reduce.1 = f32[128]{0:T(128)S(1)} all-reduce(f32[128]{0:T(128)S(1)} %dynamic-update-slice.36), channel_id=1, replica_groups=mesh['dom'=96,'sub'=8] {'sub'}, use_global_device_ids=true, to_apply=%add.1 | all-reduce | flops 128 | bytes 1024
  56.3 1.8 %fusion.30 = f32[512,1024]{1,0:T(8,128)S(1)} fusion(f32[512,128]{1,0:T(8,128)S(1)} %copy-done.32, f32[128,1024]{1,0:T(8,128)S(1)} %copy-done.2), kind=kOutput, calls=%fused_computation.117 | convolution fusion | flops 805306368 | bytes 2883584 | tf_op jit(solution)/shard_map/dot_general | solution.py:83
  58.1 0.6 fusion.9
  59.0 0.6 convolution_add_fusion.2
  59.7 0.6 convolution_add_fusion.1
  60.3 0.7 select_reduce_fusion
  61.1 0.7 fusion.1
  61.7 1.1 fusion.3
  62.8 0.6 broadcast_clamp_fusion
  63.6 1.1 copy.320
  64.8 1.1 copy.313
  66.6 13.2 %all-reduce.2 = f32[128]{0:T(128)S(1)} all-reduce(f32[128]{0:T(128)S(1)} %copy-done.52), channel_id=2, replica_groups=mesh['dom'=96,'sub'=8] {'sub'}, use_global_device_ids=true, to_apply=%region_3.4.clone | all-reduce | flops 128 | bytes 1024
  79.8 2.4 %collective-permute-start.5 = (f32[64,384]{1,0:T(8,128)S(1)}, f32[64,384]{1,0:T(8,128)S(1)}, u32[]{:S(2)}, u32[]{:S(2)}) collective-permute-start(f32[64,384]{1,0:T(8,128)S(1)} %get-tuple-element.173), channel_id=1, source_target_pairs={{24,0},{32,8},{40,16},{48,24},{56,32},{64,40},{72,48},{80,56},{88,... | collective-permute-start | bytes 294920 | tf_op jit(solution)/shard_map/ppermute | solution.py:17
  82.3 0.6 dynamic-slice_multiply_fusion
  82.9 1.0 copy.306
  83.9 1.0 copy.307
  84.9 1.0 copy.308
  85.9 1.0 copy.309
  86.9 1.0 copy.310
  87.9 5.4 %collective-permute-done.5 = f32[64,384]{1,0:T(8,128)S(1)} collective-permute-done((f32[64,384]{1,0:T(8,128)S(1)}, f32[64,384]{1,0:T(8,128)S(1)}, u32[]{:S(2)}, u32[]{:S(2)}) %collective-permute-start.5) | collective-permute-done | bytes 98336 | tf_op jit(solution)/shard_map/ppermute | solution.py:17
  93.4 1.3 stack.27
  94.8 1.5 %maximum_maximum_fusion = f32[64,8449]{1,0:T(8,128)S(1)} fusion(f32[64,2304]{1,0:T(8,128)S(1)} %bitcast.87, f32[32,6144]{1,0:T(8,128)} %copy-done.3, f32[32,6144]{1,0:T(8,128)} %copy-done.7, f32[8449]{0:T(1024)S(1)} %pad.28.clone), kind=kLoop, calls=%fused_computation.2 | loop fusion | flops 1622208 | bytes 4359428 | tf_op jit(solution)/shard_map/concatenate | solution.py:133
  96.4 3.4 %copy.311 = f32[64,8449]{0,1:T(8,128)} copy(f32[64,8449]{1,0:T(8,128)S(1)} %maximum_maximum_fusion) | data formatting | bytes 4325888 | tf_op jit(solution)/shard_map/concatenate | solution.py:133
  99.8 23.3 %gather_fusion.1 = f32[6144,64]{1,0:T(8,128)} fusion(f32[64,8449]{0,1:T(8,128)} %copy.311, s32[6144]{0:T(1024)S(1)} %copy-done.33), kind=kCustom, calls=%fused_computation.1 | custom fusion | bytes 3170304 | tf_op jit(solution)/shard_map/gather | solution.py:136
  123.1 2.4 %copy.312 = f32[6144,64]{0,1:T(8,128)S(1)} copy(f32[6144,64]{1,0:T(8,128)} %gather_fusion.1) | data formatting | bytes 3145728 | tf_op jit(solution)/shard_map/gather | solution.py:136
  125.6 2.0 %slice_add_fusion.6 = (f32[32,1024]{1,0:T(8,128)}, f32[32,1024]{1,0:T(8,128)}, f32[32,1024]{1,0:T(8,128)}, f32[32,1024]{1,0:T(8,128)}, f32[32,1024]{1,0:T(8,128)}, /*index=5*/f32[32,1024]{1,0:T(8,128)}) fusion(f32[64,6144]{1,0:T(8,128)S(1)} %bitcast.83, f32[32,1024]{1,0:T(8,128)S(1)} %copy-done.15, f32[1024]{0:T(1024)S(1)} %bitcast.98, ...), kind=kLoop, calls=%fused_computation.42 | loop fusion | flops 393216 | bytes 2371584 | tf_op jit(solution)/shard_map/add | solution.py:151
  127.7 0.9 slice_add_fusion
  128.6 0.9 reshape.566
  129.5 0.9 reshape.567
  130.5 0.9 reshape.568
  131.4 0.9 reshape.569
  132.4 0.9 reshape.570
  133.3 0.9 reshape.571
  134.4 0.2 slice_add_fusion.7
  134.6 1.0 scatter-add.54
  135.6 0.2 slice_add_fusion.5
  135.8 1.0 scatter-add.55
  137.4 0.3 copy.325
  137.8 0.2 mul.356
  138.0 0.9 add.158
  139.2 0.2 slice_add_fusion.15
  139.3 1.0 scatter-add.44
  140.4 0.2 slice_add_fusion.14
  140.6 1.0 scatter-add.45
  142.3 0.3 copy.318
  142.8 0.9 add.145
  (172 shorter events, 4.2 us)
Async XLA Ops:
  0.6 2.1 %copy-start.1 = (f32[128,1024]{1,0:T(8,128)S(1)}, f32[128,1024]{1,0:T(8,128)}, u32[]{:S(2)}) copy-start(f32[128,1024]{1,0:T(8,128)} %param.34) | copy-start | bytes 1572868
  1.9 1.8 %copy-start.49 = (f32[3,1024]{1,0:T(4,128)S(1)}, f32[3,1024]{1,0:T(4,128)}, u32[]{:S(2)}) copy-start(f32[3,1024]{1,0:T(4,128)} %param.36) | copy-start | bytes 36868
  4.3 1.1 copy-start.38
  4.3 1.1 copy-start.40
  4.3 1.1 copy-start.42
  4.3 0.7 copy-start.10
  4.4 0.7 copy-start.12
  4.5 0.7 copy-start.14
  4.6 0.7 copy-start.8
  5.4 4.1 %copy-start.3 = (f32[32,6144]{1,0:T(8,128)}, f32[32,6144]{1,0:T(8,128)S(1)}, u32[]{:S(2)}) copy-start(f32[32,6144]{1,0:T(8,128)S(1)} %neg.17) | copy-start | bytes 2359300
  5.5 0.7 copy-start.22
  5.6 0.9 copy-start.24
  6.2 0.6 copy-start.25
  6.3 0.7 copy-start.16
  6.3 0.7 copy-start.18
  6.4 0.7 copy-start.20
  7.1 2.4 %copy-start.7 = (f32[32,6144]{1,0:T(8,128)}, f32[32,6144]{1,0:T(8,128)S(1)}, u32[]{:S(2)}) copy-start(f32[32,6144]{1,0:T(8,128)S(1)} %constant_dynamic-update-slice_fusion) | copy-start | bytes 2359300
  7.2 2.3 %copy-start.48 = (s32[6,384]{1,0:T(8,128)S(1)}, s32[6,384]{1,0:T(8,128)}, u32[]{:S(2)}) copy-start(s32[6,384]{1,0:T(8,128)} %param.42) | copy-start | bytes 27652
  16.7 23.2 %copy-start.44 = (s32[6,1024]{1,0:T(8,128)S(1)}, s32[6,1024]{1,0:T(8,128)}, u32[]{:S(2)}) copy-start(s32[6,1024]{1,0:T(8,128)} %param.41) | copy-start | bytes 73732
  16.7 25.5 %copy-start.53 = (f32[16]{0:T(128)S(1)}, f32[16]{0:T(128)}, u32[]{:S(2)}) copy-start(f32[16]{0:T(128)} %param.39) | copy-start | bytes 196
  16.7 39.6 %copy-start.2 = (f32[128,1024]{1,0:T(8,128)S(1)}, f32[128,1024]{1,0:T(8,128)}, u32[]{:S(2)}) copy-start(f32[128,1024]{1,0:T(8,128)} %param.34) | copy-start | bytes 1572868
  16.7 39.6 %copy-start.32 = (f32[512,128]{1,0:T(8,128)S(1)}, f32[512,128]{1,0:T(8,128)}, u32[]{:S(2)}) copy-start(f32[512,128]{1,0:T(8,128)} %constant.306.clone) | copy-start | bytes 786436
  18.4 39.7 %copy-start = (f32[128,1024]{1,0:T(8,128)S(1)}, f32[128,1024]{1,0:T(8,128)}, u32[]{:S(2)}) copy-start(f32[128,1024]{1,0:T(8,128)} %param.35) | copy-start | bytes 1572868
  18.4 39.7 %copy-start.37 = (f32[128,128]{1,0:T(8,128)S(1)}, f32[128,128]{1,0:T(8,128)}, u32[]{:S(2)}) copy-start(f32[128,128]{1,0:T(8,128)} %constant.318) | copy-start | bytes 196612
  18.5 40.3 %copy-start.6 = (f32[128,1024]{1,0:T(8,128)S(1)}, f32[128,1024]{1,0:T(8,128)}, u32[]{:S(2)}) copy-start(f32[128,1024]{1,0:T(8,128)} %param.38) | copy-start | bytes 1572868
  18.5 61.3 %collective-permute-start = (f32[64,384]{1,0:T(8,128)S(1)}, f32[64,384]{1,0:T(8,128)}, u32[]{:S(2)}, u32[]{:S(2)}) collective-permute-start(f32[64,384]{1,0:T(8,128)S(1)} %get-tuple-element.178), channel_id=1, source_target_pairs={{0,24},{8,32},{16,40},{24,48},{32,56},{40,64},{48,72},{56,80},{64,... | collective-permute-start | bytes 294920 | tf_op jit(solution)/shard_map/ppermute | solution.py:17
  25.1 58.8 %collective-permute-start.1 = (f32[64,384]{1,0:T(8,128)S(1)}, f32[64,384]{1,0:T(8,128)}, u32[]{:S(2)}, u32[]{:S(2)}) collective-permute-start(f32[64,384]{1,0:T(8,128)S(1)} %get-tuple-element.177), channel_id=1, source_target_pairs={{0,16},{8,24},{16,32},{24,40},{32,48},{40,56},{48,64},{56,72},{64,... | collective-permute-start | bytes 294920 | tf_op jit(solution)/shard_map/ppermute | solution.py:17
  27.5 57.4 %collective-permute-start.2 = (f32[64,384]{1,0:T(8,128)S(1)}, f32[64,384]{1,0:T(8,128)}, u32[]{:S(2)}, u32[]{:S(2)}) collective-permute-start(f32[64,384]{1,0:T(8,128)S(1)} %get-tuple-element.176), channel_id=1, source_target_pairs={{0,8},{8,16},{16,24},{24,32},{32,40},{40,48},{48,56},{56,64},{64,7... | collective-permute-start | bytes 294920 | tf_op jit(solution)/shard_map/ppermute | solution.py:17
  29.8 56.0 %collective-permute-start.3 = (f32[64,384]{1,0:T(8,128)S(1)}, f32[64,384]{1,0:T(8,128)}, u32[]{:S(2)}, u32[]{:S(2)}) collective-permute-start(f32[64,384]{1,0:T(8,128)S(1)} %get-tuple-element.175), channel_id=1, source_target_pairs={{8,0},{16,8},{24,16},{32,24},{40,32},{48,40},{56,48},{64,56},{72,6... | collective-permute-start | bytes 294920 | tf_op jit(solution)/shard_map/ppermute | solution.py:17
  32.8 54.1 %collective-permute-start.4 = (f32[64,384]{1,0:T(8,128)S(1)}, f32[64,384]{1,0:T(8,128)}, u32[]{:S(2)}, u32[]{:S(2)}) collective-permute-start(f32[64,384]{1,0:T(8,128)S(1)} %get-tuple-element.174), channel_id=1, source_target_pairs={{16,0},{24,8},{32,16},{40,24},{48,32},{56,40},{64,48},{72,56},{80,... | collective-permute-start | bytes 294920 | tf_op jit(solution)/shard_map/ppermute | solution.py:17
  39.9 21.1 %copy-start.50 = (f32[128]{0:T(128)}, f32[128]{0:T(128)S(1)}, u32[]{:S(2)}) copy-start(f32[128]{0:T(128)S(1)} %compare_select_fusion.2) | copy-start | bytes 1540
  56.3 2.7 %copy-start.36 = (f32[128,128]{1,0:T(8,128)S(1)}, f32[128,128]{1,0:T(8,128)}, u32[]{:S(2)}) copy-start(f32[128,128]{1,0:T(8,128)} %constant.319) | copy-start | bytes 196612
  56.3 2.7 %copy-start.47 = (f32[1,1024]{1,0:T(1,128)S(1)}, f32[1,1024]{1,0:T(1,128)}, u32[]{:S(2)}) copy-start(f32[1,1024]{1,0:T(1,128)} %get-tuple-element.190) | copy-start | bytes 12292
  58.1 1.6 %copy-start.35 = (f32[128,128]{1,0:T(8,128)S(1)}, f32[128,128]{1,0:T(8,128)}, u32[]{:S(2)}) copy-start(f32[128,128]{1,0:T(8,128)} %constant.320) | copy-start | bytes 196612
  58.8 1.5 %copy-start.51 = (s32[1024]{0:T(1024)S(1)}, s32[1024]{0:T(1024)}, u32[]{:S(2)}) copy-start(s32[1024]{0:T(1024)} %param.40) | copy-start | bytes 12292
  58.8 2.3 %copy-start.34 = (f32[128,128]{1,0:T(8,128)S(1)}, f32[128,128]{1,0:T(8,128)}, u32[]{:S(2)}) copy-start(f32[128,128]{1,0:T(8,128)} %constant.321) | copy-start | bytes 196612
  58.8 2.3 %copy-start.45 = (f32[1024]{0:T(1024)S(1)}, f32[1024]{0:T(1024)}, u32[]{:S(2)}) copy-start(f32[1024]{0:T(1024)} %param.37) | copy-start | bytes 12292
  59.6 2.1 %copy-start.46 = (f32[1,1024]{1,0:T(1,128)S(1)}, f32[1,1024]{1,0:T(1,128)}, u32[]{:S(2)}) copy-start(f32[1,1024]{1,0:T(1,128)} %get-tuple-element.197) | copy-start | bytes 12292
  62.8 3.8 %copy-start.52 = (f32[128]{0:T(128)S(1)}, f32[128]{0:T(128)}, u32[]{:S(2)}) copy-start(f32[128]{0:T(128)} %get-tuple-element.151) | copy-start | bytes 1540
  79.8 13.5 %collective-permute-start.5 = (f32[64,384]{1,0:T(8,128)S(1)}, f32[64,384]{1,0:T(8,128)S(1)}, u32[]{:S(2)}, u32[]{:S(2)}) collective-permute-start(f32[64,384]{1,0:T(8,128)S(1)} %get-tuple-element.173), channel_id=1, source_target_pairs={{24,0},{32,8},{40,16},{48,24},{56,32},{64,40},{72,48},{80,56},{88,... | collective-permute-start | bytes 294920 | tf_op jit(solution)/shard_map/ppermute | solution.py:17
  96.3 3.4 %copy-start.33 = (s32[6144]{0:T(1024)S(1)}, s32[6144]{0:T(1024)}, u32[]{:S(2)}) copy-start(s32[6144]{0:T(1024)} %broadcast_clamp_fusion) | copy-start | bytes 73732
  123.0 2.5 %copy-start.11 = (f32[32,1024]{1,0:T(8,128)S(1)}, f32[32,1024]{1,0:T(8,128)}, u32[]{:S(2)}) copy-start(f32[32,1024]{1,0:T(8,128)} %copy-done.10) | copy-start | bytes 393220
  123.0 2.5 %copy-start.13 = (f32[32,1024]{1,0:T(8,128)S(1)}, f32[32,1024]{1,0:T(8,128)}, u32[]{:S(2)}) copy-start(f32[32,1024]{1,0:T(8,128)} %copy-done.12) | copy-start | bytes 393220
  123.0 2.5 %copy-start.15 = (f32[32,1024]{1,0:T(8,128)S(1)}, f32[32,1024]{1,0:T(8,128)}, u32[]{:S(2)}) copy-start(f32[32,1024]{1,0:T(8,128)} %copy-done.14) | copy-start | bytes 393220
  123.0 2.5 %copy-start.23 = (f32[32,1024]{1,0:T(8,128)S(1)}, f32[32,1024]{1,0:T(8,128)}, u32[]{:S(2)}) copy-start(f32[32,1024]{1,0:T(8,128)} %copy-done.22) | copy-start | bytes 393220
  123.0 2.5 %copy-start.39 = (f32[1,1024]{1,0:T(1,128)S(1)}, f32[1,1024]{1,0:T(1,128)}, u32[]{:S(2)}) copy-start(f32[1,1024]{1,0:T(1,128)} %copy-done.38) | copy-start | bytes 12292
  123.1 2.5 %copy-start.41 = (f32[1,1024]{1,0:T(1,128)S(1)}, f32[1,1024]{1,0:T(1,128)}, u32[]{:S(2)}) copy-start(f32[1,1024]{1,0:T(1,128)} %copy-done.40) | copy-start | bytes 12292
  123.1 2.5 %copy-start.43 = (f32[1,1024]{1,0:T(1,128)S(1)}, f32[1,1024]{1,0:T(1,128)}, u32[]{:S(2)}) copy-start(f32[1,1024]{1,0:T(1,128)} %copy-done.42) | copy-start | bytes 12292
  125.5 2.1 %copy-start.9 = (f32[32,1024]{1,0:T(8,128)S(1)}, f32[32,1024]{1,0:T(8,128)}, u32[]{:S(2)}) copy-start(f32[32,1024]{1,0:T(8,128)} %copy-done.8) | copy-start | bytes 393220
  125.5 2.1 %copy-start.17 = (f32[32,1024]{1,0:T(8,128)S(1)}, f32[32,1024]{1,0:T(8,128)}, u32[]{:S(2)}) copy-start(f32[32,1024]{1,0:T(8,128)} %copy-done.16) | copy-start | bytes 393220
  125.5 2.1 %copy-start.19 = (f32[32,1024]{1,0:T(8,128)S(1)}, f32[32,1024]{1,0:T(8,128)}, u32[]{:S(2)}) copy-start(f32[32,1024]{1,0:T(8,128)} %copy-done.18) | copy-start | bytes 393220
  125.5 2.1 %copy-start.21 = (f32[32,1024]{1,0:T(8,128)S(1)}, f32[32,1024]{1,0:T(8,128)}, u32[]{:S(2)}) copy-start(f32[32,1024]{1,0:T(8,128)} %copy-done.20) | copy-start | bytes 393220
  127.6 6.6 %copy-start.5 = (f32[2,4,4,4,1024]{4,2,1,0,3:T(4,128)S(1)}, f32[2,4,4,4,1024]{4,2,1,0,3:T(4,128)}, u32[]{:S(2)}) copy-start(f32[2,4,4,4,1024]{4,2,1,0,3:T(4,128)} %copy.320) | copy-start | bytes 1572868
  137.2 1.6 %copy-start.31 = (f32[32,1024]{1,0:T(8,128)S(1)}, f32[32,1024]{1,0:T(8,128)}, u32[]{:S(2)}) copy-start(f32[32,1024]{1,0:T(8,128)} %get-tuple-element.167) | copy-start | bytes 393220
  137.4 1.5 %copy-start.30 = (f32[32,1024]{1,0:T(8,128)S(1)}, f32[32,1024]{1,0:T(8,128)}, u32[]{:S(2)}) copy-start(f32[32,1024]{1,0:T(8,128)} %get-tuple-element.171) | copy-start | bytes 393220
  137.4 1.6 %copy-start.29 = (f32[32,1024]{1,0:T(8,128)S(1)}, f32[32,1024]{1,0:T(8,128)}, u32[]{:S(2)}) copy-start(f32[32,1024]{1,0:T(8,128)} %get-tuple-element.169) | copy-start | bytes 393220
  137.4 1.6 %copy-start.28 = (f32[32,1024]{1,0:T(8,128)S(1)}, f32[32,1024]{1,0:T(8,128)}, u32[]{:S(2)}) copy-start(f32[32,1024]{1,0:T(8,128)} %get-tuple-element.160) | copy-start | bytes 393220
  137.4 1.6 %copy-start.4 = (f32[2,4,4,4,1024]{4,2,1,0,3:T(4,128)S(1)}, f32[2,4,4,4,1024]{4,2,1,0,3:T(4,128)}, u32[]{:S(2)}) copy-start(f32[2,4,4,4,1024]{4,2,1,0,3:T(4,128)} %copy.313) | copy-start | bytes 1572868
  137.9 3.7 %copy-start.27 = (f32[32,1024]{1,0:T(8,128)S(1)}, f32[32,1024]{1,0:T(8,128)}, u32[]{:S(2)}) copy-start(f32[32,1024]{1,0:T(8,128)} %get-tuple-element.165) | copy-start | bytes 393220
  138.0 3.8 %copy-start.26 = (f32[32,1024]{1,0:T(8,128)S(1)}, f32[32,1024]{1,0:T(8,128)}, u32[]{:S(2)}) copy-start(f32[32,1024]{1,0:T(8,128)} %get-tuple-element.154) | copy-start | bytes 393220
where the time goes:
time: 144 us
  local copies, waits for them, and re-layouts  67.6 us (47%)
  blocking collectives  27 us (19%)
  starting transfers between devices  23.8 us (17%)
  other arithmetic  12.2 us (8%)
  waiting for transfers between devices  5.44 us (4%)
  matrix products  4.38 us (3%)
  between operations  3.28 us (2%)
    unnamed x2, blocking collectives  27 us
    gather x2, local copies, waits for them, and re-layouts, finish(): picked = full_table[:, face_source.reshape(-1)]  25.7 us
    ppermute x6, starting transfers between devices, shifted(): return lax.ppermute(block, axis, route)  23.8 us
    gather x2, local copies, waits for them, and re-layouts, outgoing(): send_both = own_table[:, send_face]  6.76 us
    another operation x7, local copies, waits for them, and re-layouts, shards(): arrived_both = jnp.stack(arrived, axis=1)  6.35 us
    unnamed x123, local copies, waits for them, and re-layouts  6.15 us
    another operation x12, local copies, waits for them, and re-layouts  5.89 us
    ppermute x6, waiting for transfers between devices, shifted(): return lax.ppermute(block, axis, route)  5.44 us
  transfers between devices with their start and end apart: 6, of which 1 were waited for; matrix products, arithmetic and copies ran while one was open for 12% of the time, Pallas kernels for 0%

commit v1 on v0

v1 whole, which is shorter than its diff:
```python
import functools

import jax
import jax.numpy as jnp
import numpy as np
from jax import lax
from jax.experimental import pallas as pl
from jax.experimental.pallas import tpu as pltpu
from jax.sharding import PartitionSpec as P

REACH = 3
ROUNDS = 2 * REACH
STEP = 0.02
SECOND_SPECIES = 0.35
ELEMS = 1024
FACES = 6 * ELEMS
CAP = 384
HALF = CAP // 2
TABLE = FACES + ROUNDS * CAP + 8
N_SUB = 8
BLOCKS = 128
MESH = pl.DeviceIdType.MESH
F32 = jnp.float32
BF16 = jnp.bfloat16


def nodal_matrices():
    inner_point = 1.0 / np.sqrt(5.0)
    points = np.array([-1.0, -inner_point, inner_point, 1.0])
    bary_weight = np.array(
        [1.0 / np.prod([points[j] - points[m] for m in range(4) if m != j]) for j in range(4)]
    )
    derivative = np.zeros((4, 4))
    for i in range(4):
        for j in range(4):
            if i != j:
                derivative[i, j] = bary_weight[j] / bary_weight[i] / (points[i] - points[j])
        derivative[i, i] = -np.sum(derivative[i])
    identity = np.eye(4)
    along_i = np.kron(identity, np.kron(identity, derivative))
    along_j = np.kron(identity, np.kron(derivative, identity))
    along_k = np.kron(derivative, np.eye(16))
    second = along_i @ along_i + along_j @ along_j + along_k @ along_k
    return [np.kron(np.eye(2), matrix) for matrix in (along_i, along_j, along_k, second)]


def split_constant(matrices):
    stacked = np.concatenate(matrices, axis=0).astype(np.float32)
    high = stacked.astype(BF16)
    low = (stacked - high.astype(np.float32)).astype(BF16)
    return np.concatenate([high, high, low], axis=1)


def face_rows(face):
    rows = []
    for species in range(2):
        for slow in range(4):
            for fast in range(4):
                direction, last = face // 2, 3 * (face % 2)
                if direction == 0:
                    node = last + 4 * fast + 16 * slow
                elif direction == 1:
                    node = fast + 4 * last + 16 * slow
                else:
                    node = fast + 4 * slow + 16 * last
                rows.append(species * 64 + node)
    return rows


def face_expansion():
    expand = np.zeros((128, 192), np.float32)
    for face in range(6):
        for place, row in enumerate(face_rows(face)):
            expand[row, face * 32 + place] = 1.0
    return np.concatenate([expand, expand], axis=1).astype(BF16)


def split2(x):
    high = x.astype(BF16)
    return high, (x - high.astype(F32)).astype(BF16)


def split3(x):
    high, rest = x.astype(BF16), None
    rest = x - high.astype(F32)
    middle = rest.astype(BF16)
    return high, middle, (rest - middle.astype(F32)).astype(BF16)


def iota(shape, axis):
    return lax.broadcasted_iota(jnp.int32, shape, axis)


def trace_of(ref, face, chunk):
    direction, upper = face // 2, face % 2
    if direction == 0:
        return ref[chunk, pl.ds(3 * upper, 32, stride=4), :]
    if direction == 2:
        start = 48 * upper
        return jnp.concatenate(
            [ref[chunk, pl.ds(start, 16), :], ref[chunk, pl.ds(64 + start, 16), :]], axis=0
        )
    low_half = iota((8, 128), 0) < 4
    pieces = []
    for n in range(0, 8, 2):
        if upper == 0:
            first = ref[chunk, pl.ds(16 * n, 8), :]
            second = ref[chunk, pl.ds(16 * (n + 1) - 4, 8), :]
        else:
            first = ref[chunk, pl.ds(16 * n + 12, 8), :]
            second = ref[chunk, pl.ds(16 * (n + 1) + 8, 8), :]
        pieces.append(jnp.where(low_half, first, second))
    return jnp.concatenate(pieces, axis=0)


def face_weight(velocity, face):
    normal = velocity[face // 2 : face // 2 + 1]
    return 6.0 * jnp.minimum(normal if face % 2 else -normal, 0.0)


def expand_faces(pair_rows, velocity, expansion):
    outer_parts, back_parts = [], []
    for pair in range(3):
        columns = jnp.transpose(pair_rows(pair))
        for side in range(2):
            weight = face_weight(velocity, 2 * pair + side) * (-STEP)
            outer_parts.append(columns[64 * side : 64 * side + 32] * weight)
            back_parts.append(columns[64 * side + 32 : 64 * side + 64] * STEP)
    terms = jnp.concatenate(
        [jnp.concatenate(outer_parts, axis=0), jnp.concatenate(back_parts, axis=0)], axis=1
    )
    high, low = split2(terms)
    added = jnp.dot(
        expansion, jnp.concatenate([high, low], axis=0), preferred_element_type=F32
    )
    return added[:, :128], added[:, 128:]


def exchange_kernel(
    n_dom,
    state_hbm,
    cotangent_hbm,
    velocity_hbm,
    dispersion_hbm,
    retained_hbm,
    kappa_hbm,
    block_hbm,
    source_hbm,
    send_hbm,
    forward_hbm,
    backward_hbm,
    expansion_hbm,
    advanced,
    adjoint,
    arrived_out,
    sums_out,
    state,
    cotangent,
    velocity,
    dispersion,
    retained,
    block,
    forward_op,
    backward_op,
    expansion,
    kappa_ref,
    source_index,
    send_index,
    table,
    pairs,
    outgoing,
    kappa_rows,
    sums_row,
    sums_acc,
    in_sem,
    field_sem,
    index_sem,
    send_sem,
    recv_sem,
    kappa_send,
    kappa_recv,
    sums_send,
    sums_recv,
):
    dom = lax.axis_index("dom")
    sub = lax.axis_index("sub")
    loads = {}
    for number, (name, src, dst) in enumerate(
        [
            ("velocity", velocity_hbm, velocity),
            ("kappa", kappa_hbm, kappa_ref),
            ("block", block_hbm, block),
            ("dispersion", dispersion_hbm, dispersion),
            ("forward", forward_hbm, forward_op),
            ("backward", backward_hbm, backward_op),
            ("expansion", expansion_hbm, expansion),
        ]
    ):
        loads[name] = pltpu.make_async_copy(src, dst, in_sem.at[number])
    send_loads = [
        pltpu.make_async_copy(
            send_hbm.at[number], send_index.at[pl.ds(number * CAP, CAP)], index_sem.at[number]
        )
        for number in range(ROUNDS)
    ]
    source_loads = [
        pltpu.make_async_copy(
            source_hbm.at[face],
            source_index.at[pl.ds(face * ELEMS, ELEMS)],
            index_sem.at[ROUNDS + face],
        )
        for face in range(6)
    ]

    def field_load(number, chunk):
        src, dst = ((state_hbm, state), (cotangent_hbm, cotangent), (retained_hbm, retained))[number]
        start = chunk * 128 if isinstance(chunk, int) else pl.multiple_of(chunk * 128, 128)
        return pltpu.make_async_copy(
            src.at[:, pl.ds(start, 128)], dst.at[chunk], field_sem.at[number, chunk]
        )

    loads["velocity"].start()
    loads["kappa"].start()
    for chunk in range(ELEMS // 128):
        for number in range(2):
            field_load(number, chunk).start()
    for load in send_loads:
        load.start()
    for load in source_loads:
        load.start()
    for chunk in range(ELEMS // 128):
        field_load(2, chunk).start()
    for name in ("block", "dispersion", "forward", "backward", "expansion"):
        loads[name].start()

    def dom_partner(offset):
        return lax.rem(dom + (offset + n_dom), n_dom)

    def sub_partner(turn):
        return lax.rem(sub + turn, N_SUB)

    offsets = [n - REACH if n < REACH else n - REACH + 1 for n in range(ROUNDS)]
    barrier = pltpu.get_barrier_semaphore()
    for offset in offsets:
        pl.semaphore_signal(
            barrier, inc=1, device_id={"dom": dom_partner(offset)}, device_id_type=MESH
        )
    for turn in range(1, N_SUB):
        pl.semaphore_signal(
            barrier, inc=1, device_id={"sub": sub_partner(turn)}, device_id_type=MESH
        )

    zero_tile = jnp.zeros((8, 128), F32)

    def clear(step, carry):
        table[pl.ds(pl.multiple_of(FACES + step * 8, 8), 8), :] = zero_tile
        return carry

    lax.fori_loop(0, (TABLE - FACES) // 8, clear, 0, unroll=17)

    lane_row = iota((1, 128), 1)
    own_row = jnp.zeros((1, 128), F32)
    loads["kappa"].wait()
    for place in range(16):
        own_row = jnp.where(lane_row == sub * 16 + place, kappa_ref[place], own_row)
    kappa_rows[0] = own_row

    loads["velocity"].wait()
    low_lanes = iota((128, 128), 1) < 64

    def build(chunk, carry):
        field_load(0, chunk).wait()
        field_load(1, chunk).wait()
        start = pl.multiple_of(chunk * 128, 128)
        cols = pl.ds(start, 128)
        speeds = velocity[:, cols]
        for pair in range(3):
            parts = []
            for face in (2 * pair, 2 * pair + 1):
                parts.append(trace_of(state, face, chunk))
                parts.append(trace_of(cotangent, face, chunk) * (-face_weight(speeds, face)))
            rows = jnp.transpose(jnp.concatenate(parts, axis=0))
            turned = pltpu.roll(rows, 64, 1)
            table[pl.ds(pl.multiple_of(2 * pair * ELEMS + start, 128), 128), :] = jnp.where(
                low_lanes, rows, turned
            )
            table[pl.ds(pl.multiple_of((2 * pair + 1) * ELEMS + start, 128), 128), :] = jnp.where(
                low_lanes, turned, rows
            )
        return carry

    lax.fori_loop(0, ELEMS // 128, build, 0)
    low_row = iota((1, 128), 1) < 64

    for load in send_loads:
        load.wait()
    pl.semaphore_wait(barrier, ROUNDS + N_SUB - 1)

    kappa_copies = [
        pltpu.make_async_remote_copy(
            src_ref=kappa_rows.at[0],
            dst_ref=kappa_rows.at[turn],
            send_sem=kappa_send.at[turn],
            recv_sem=kappa_recv.at[turn],
            device_id={"sub": sub_partner(turn)},
            device_id_type=MESH,
        )
        for turn in range(1, N_SUB)
    ]
    for copy in kappa_copies:
        copy.start()

    group = 32
    round_copies = []
    for number in (0, 5, 1, 4, 2, 3):

        def gather(step, carry, number=number):
            base = step * group
            values = []
            for place in range(group):
                first = send_index[number * CAP + base + place]
                second = send_index[number * CAP + HALF + base + place]
                values.append(
                    jnp.where(low_row, table[pl.ds(first, 1), :], table[pl.ds(second, 1), :])
                )
            for place in range(group):
                outgoing[number, pl.ds(base + place, 1), :] = values[place]
            return carry

        lax.fori_loop(0, HALF // group, gather, 0)
        copy = pltpu.make_async_remote_copy(
            src_ref=outgoing.at[number],
            dst_ref=arrived_out.at[ROUNDS - 1 - number],
            send_sem=send_sem.at[number],
            recv_sem=recv_sem.at[ROUNDS - 1 - number],
            device_id={"dom": dom_partner(offsets[number])},
            device_id_type=MESH,
        )
        copy.start()
        round_copies.append(copy)

    for copy in kappa_copies:
        copy.wait_recv()
    slab = kappa_rows[0]
    for turn in range(1, N_SUB):
        slab = slab + kappa_rows[turn]
    slab_parts = jnp.concatenate(
        list(split3(slab)) + [jnp.zeros((13, 128), BF16)], axis=0
    )
    for name in ("block", "dispersion", "forward", "backward"):
        loads[name].wait()
    for chunk in range(ELEMS // 128):
        field_load(2, chunk).wait()
    sums_acc[...] = jnp.zeros_like(sums_acc)

    width = 256
    sublane = iota((8, width), 0)

    def volume(chunk, carry):
        start = pl.multiple_of(chunk * width, width)
        cols = pl.ds(start, width)
        hits = (iota((BLOCKS, width), 0) == block[:, cols]).astype(F32).astype(BF16)
        rates = jnp.dot(slab_parts, hits, preferred_element_type=F32)
        elem_rate = (rates[0:1] + rates[1:2]) + rates[2:3]
        speeds = velocity[:, cols]
        spread = dispersion[:, cols] * STEP

        def two_chunks(ref):
            return jnp.concatenate([ref[2 * chunk], ref[2 * chunk + 1]], axis=1)

        field = two_chunks(state)
        dual = two_chunks(cotangent)
        weights = [face_weight(speeds, face) for face in range(6)]
        along_i = jnp.where(
            sublane % 4 == 0, weights[0], jnp.where(sublane % 4 == 3, weights[1], 0.0)
        )
        by_j = [
            along_i + jnp.where(sublane < 4, weights[2], 0.0),
            along_i + jnp.where(sublane >= 4, weights[3], 0.0),
        ]
        tiles = [by_j[0] + weights[4], by_j[1] + weights[4]]
        tiles += [by_j[0], by_j[1], by_j[0], by_j[1]]
        tiles += [by_j[0] + weights[5], by_j[1] + weights[5]]
        face_part = jnp.concatenate(tiles + tiles, axis=0)
        gain = jnp.where(iota((128, width), 0) < 64, 1.0, SECOND_SPECIES)
        free = gain * (1.0 - two_chunks(retained))
        factor = 1.0 + STEP * (face_part - elem_rate * free)
        terms = jnp.sum(free * dual * field, axis=0, keepdims=True)
        term_parts = jnp.concatenate(
            list(split3(terms)) + [jnp.zeros((13, width), BF16)], axis=0
        )
        sums_acc[...] += lax.dot_general(
            term_parts, hits, (((1,), (1,)), ((), ())), preferred_element_type=F32
        )
        for values, operator, target in (
            (field, forward_op, advanced),
            (dual, backward_op, adjoint),
        ):
            high, low = split2(values)
            images = jnp.dot(
                operator[...],
                jnp.concatenate([high, low, high], axis=0),
                preferred_element_type=F32,
            )
            target[:, cols] = (
                factor * values
                - (STEP * speeds[0:1]) * images[0:128]
                - (STEP * speeds[1:2]) * images[128:256]
                - (STEP * speeds[2:3]) * images[256:384]
                + spread * images[384:512]
            )
        return carry

    lax.fori_loop(0, ELEMS // width, volume, 0)
    sums_row[...] = (sums_acc[0:1] + sums_acc[1:2]) + sums_acc[2:3]

    sums_out[0] = sums_row[...]
    sums_copies = [
        pltpu.make_async_remote_copy(
            src_ref=sums_row,
            dst_ref=sums_out.at[turn],
            send_sem=sums_send.at[turn],
            recv_sem=sums_recv.at[turn],
            device_id={"sub": sub_partner(turn)},
            device_id_type=MESH,
        )
        for turn in range(1, N_SUB)
    ]
    for copy in sums_copies:
        copy.start()

    for load in source_loads:
        load.wait()
    for pair in range(3):

        def pick(step, carry, pair=pair):
            base = step * group
            values = []
            for place in range(group):
                first = source_index[2 * pair * ELEMS + base + place]
                second = source_index[(2 * pair + 1) * ELEMS + base + place]
                values.append(
                    jnp.where(low_row, table[pl.ds(first, 1), :], table[pl.ds(second, 1), :])
                )
            for place in range(group):
                pairs[pl.ds(pair * ELEMS + base + place, 1), :] = values[place]
            return carry

        lax.fori_loop(0, ELEMS // group, pick, 0)

    loads["expansion"].wait()

    def close(chunk, carry):
        start = pl.multiple_of(chunk * 128, 128)
        cols = pl.ds(start, 128)
        added = expand_faces(
            lambda pair: pairs[pl.ds(pl.multiple_of(pair * ELEMS + start, 128), 128), :],
            velocity[:, cols],
            expansion[...],
        )
        advanced[:, cols] += added[0]
        adjoint[:, cols] += added[1]
        return carry

    lax.fori_loop(0, ELEMS // 128, close, 0)
    for copy in kappa_copies:
        copy.wait_send()
    for copy in sums_copies:
        copy.wait()
    for copy in round_copies:
        copy.wait()


def merge_kernel(
    part_advanced,
    part_adjoint,
    arrived,
    sums,
    velocity_hbm,
    send_hbm,
    expansion_hbm,
    advanced_out,
    adjoint_out,
    grad_out,
    advanced,
    adjoint,
    velocity,
    expansion,
    send_index,
    rows,
    spread,
    in_sem,
    index_sem,
    out_sem,
):
    sub = lax.axis_index("sub")
    loads = [
        pltpu.make_async_copy(src, dst, in_sem.at[number])
        for number, (src, dst) in enumerate(
            [
                (velocity_hbm, velocity),
                (expansion_hbm, expansion),
            ]
        )
    ]
    index_loads = [
        pltpu.make_async_copy(
            send_hbm.at[number], send_index.at[pl.ds(number * CAP, CAP)], index_sem.at[number]
        )
        for number in range(ROUNDS)
    ]
    for load in index_loads:
        load.start()
    for load in loads:
        load.start()
    zero_tile = jnp.zeros((8, 128), F32)

    def clear(step, carry):
        for place in range(16):
            spread[pl.ds(pl.multiple_of(step * 128 + place * 8, 8), 8), :] = zero_tile
        return carry

    lax.fori_loop(0, FACES // 128, clear, 0)
    low_lanes = iota((HALF, 128), 1) < 64
    for number in range(ROUNDS):
        values = arrived[number]
        turned = pltpu.roll(values, 64, 1)
        rows[pl.ds(number * CAP, HALF), :] = jnp.where(low_lanes, values, turned)
        rows[pl.ds(number * CAP + HALF, HALF), :] = jnp.where(low_lanes, turned, values)
    for load in index_loads:
        load.wait()
    group = 64

    def scatter(step, carry):
        base = step * group
        values = [rows[pl.ds(base + place, 1), :] for place in range(group)]
        for place in range(group):
            spread[pl.ds(send_index[base + place], 1), :] = values[place]
        return carry

    lax.fori_loop(0, ROUNDS * CAP // group, scatter, 0)
    for load in loads:
        load.wait()
    total = jnp.zeros((1, 128), F32)
    for turn in range(N_SUB):
        total = total + sums[turn]
    total = pltpu.roll(total, 128 - sub * 16, 1)
    grad_out[...] = -STEP * total[:, :16]
    low_part = iota((128, 128), 1) < 64

    def results(chunk):
        cols = pl.ds(pl.multiple_of(chunk * 128, 128), 128)
        return [
            pltpu.make_async_copy(
                advanced.at[:, cols], advanced_out.at[:, cols], out_sem.at[0, chunk]
            ),
            pltpu.make_async_copy(
                adjoint.at[:, cols], adjoint_out.at[:, cols], out_sem.at[1, chunk]
            ),
        ]

    def close(chunk, carry):
        start = pl.multiple_of(chunk * 128, 128)
        cols = pl.ds(start, 128)

        def pair_rows(pair):
            first = spread[pl.ds(pl.multiple_of(2 * pair * ELEMS + start, 128), 128), :]
            second = spread[pl.ds(pl.multiple_of((2 * pair + 1) * ELEMS + start, 128), 128), :]
            return jnp.where(low_part, first, second)

        added = expand_faces(pair_rows, velocity[:, cols], expansion[...])
        advanced[:, cols] = part_advanced[:, cols] + added[0]
        adjoint[:, cols] = part_adjoint[:, cols] + added[1]
        for copy in results(chunk):
            copy.start()
        return carry

    lax.fori_loop(0, ELEMS // 128, close, 0)

    def finish(chunk, carry):
        for copy in results(chunk):
            copy.wait()
        return carry

    lax.fori_loop(0, ELEMS // 128, finish, 0)


def solution(mesh):
    n_dom = mesh.shape["dom"]
    matrices = nodal_matrices()
    forward_np = split_constant(matrices)
    backward_np = split_constant([matrix.T for matrix in matrices])
    expansion_np = face_expansion()
    in_hbm = pl.BlockSpec(memory_space=pltpu.HBM)
    in_vmem = pl.BlockSpec(memory_space=pltpu.VMEM)
    dma = pltpu.SemaphoreType.DMA
    field = jax.ShapeDtypeStruct((128, ELEMS), F32)

    def shards(
        state, cotangent, velocity, dispersion, retained, kappa, elem_block, face_source, send_face
    ):
        kept = functools.partial(pltpu.with_memory_space_constraint, memory_space=pltpu.HBM)
        forward_op = kept(jnp.asarray(forward_np))
        backward_op = kept(jnp.asarray(backward_np))
        expansion = kept(jnp.asarray(expansion_np))
        state, cotangent, velocity, retained = map(kept, (state, cotangent, velocity, retained))
        face_source, send_face, kappa = map(kept, (face_source, send_face, kappa))
        dispersion = kept(dispersion.reshape(1, ELEMS))
        elem_block = kept(elem_block.reshape(1, ELEMS))
        part_advanced, part_adjoint, arrived, sums = pl.pallas_call(
            functools.partial(exchange_kernel, n_dom),
            out_shape=(
                field,
                field,
                jax.ShapeDtypeStruct((ROUNDS, HALF, 128), F32),
                jax.ShapeDtypeStruct((N_SUB, 1, 128), F32),
            ),
            in_specs=[in_hbm] * 12,
            out_specs=(in_vmem,) * 4,
            scratch_shapes=[
                pltpu.VMEM((ELEMS // 128, 128, 128), F32),
                pltpu.VMEM((ELEMS // 128, 128, 128), F32),
                pltpu.VMEM((3, ELEMS), F32),
                pltpu.VMEM((1, ELEMS), F32),
                pltpu.VMEM((ELEMS // 128, 128, 128), F32),
                pltpu.VMEM((1, ELEMS), jnp.int32),
                pltpu.VMEM((512, 384), BF16),
                pltpu.VMEM((512, 384), BF16),
                pltpu.VMEM((128, 384), BF16),
                pltpu.SMEM((16,), F32),
                pltpu.SMEM((FACES,), jnp.int32),
                pltpu.SMEM((ROUNDS * CAP,), jnp.int32),
                pltpu.VMEM((TABLE, 128), F32),
                pltpu.VMEM((3 * ELEMS, 128), F32),
                pltpu.VMEM((ROUNDS, HALF, 128), F32),
                pltpu.VMEM((N_SUB, 1, 128), F32),
                pltpu.VMEM((1, 128), F32),
                pltpu.VMEM((16, 128), F32),
                dma((7,)),
                dma((3, ELEMS // 128)),
                dma((ROUNDS + 6,)),
                dma((ROUNDS,)),
                dma((ROUNDS,)),
                dma((N_SUB,)),
                dma((N_SUB,)),
                dma((N_SUB,)),
                dma((N_SUB,)),
            ],
            compiler_params=pltpu.CompilerParams(
                collective_id=0, has_side_effects=True, vmem_limit_bytes=40 << 20
            ),
            name="exchange",
        )(
            state,
            cotangent,
            velocity,
            dispersion,
            retained,
            kappa,
            elem_block,
            face_source,
            send_face,
            forward_op,
            backward_op,
            expansion,
        )
        advanced, adjoint, grad = pl.pallas_call(
            merge_kernel,
            out_shape=(field, field, jax.ShapeDtypeStruct((1, 16), F32)),
            in_specs=[in_vmem] * 4 + [in_hbm] * 3,
            out_specs=(in_hbm, in_hbm, in_vmem),
            scratch_shapes=[
                pltpu.VMEM((128, ELEMS), F32),
                pltpu.VMEM((128, ELEMS), F32),
                pltpu.VMEM((3, ELEMS), F32),
                pltpu.VMEM((128, 384), BF16),
                pltpu.SMEM((ROUNDS * CAP,), jnp.int32),
                pltpu.VMEM((ROUNDS * CAP, 128), F32),
                pltpu.VMEM((FACES + 8, 128), F32),
                dma((2,)),
                dma((ROUNDS,)),
                dma((2, ELEMS // 128)),
            ],
            compiler_params=pltpu.CompilerParams(vmem_limit_bytes=40 << 20),
            name="merge",
        )(part_advanced, part_adjoint, arrived, sums, velocity, send_face, expansion)
        return advanced, adjoint, grad.reshape(16)

    wide = P(None, ("dom", "sub"))
    flat = P(("dom", "sub"))
    return jax.shard_map(
        shards,
        mesh=mesh,
        in_specs=(wide, wide, wide, flat, wide, flat, flat, wide, wide),
        out_specs=(wide, wide, flat),
        check_vma=False,
    )
```

time: 144 us -> 42.1 us (0.29)
  the two profiles are of different devices: /device:TPU:521 before, /device:TPU:1 now
where the time goes in v1:
time: 42.1 us; the launch traced here: 42 us
  Pallas kernels  41.3 us (98%)
  between operations  0.64 us (2%)
    pallas_call x1, Pallas kernels, shards(): pl.pallas_call(functools.partial(exchange_kernel, n_dom), out_shape=(fiel...  34.5 us
    pallas_call x1, Pallas kernels, shards(): pl.pallas_call(merge_kernel, out_shape=(field, field, jax.ShapeDtypeStruc...  6.82 us

profile of v1, /device:TPU:1, one launch (start us, length us, event | category | flops | bytes accessed | tf_op | source)
XLA Modules:
  0.0 42.0 jit_solution(3733368519509444777)
XLA Ops:
  0.6 34.5 %exchange.1 = (f32[128,1024]{1,0:T(8,128)S(1)}, f32[128,1024]{1,0:T(8,128)S(1)}, f32[6,192,128]{2,1,0:T(8,128)S(1)}, f32[8,1,128]{2,1,0:T(1,128)S(1)}) custom-call(f32[128,1024]{1,0:T(8,128)} %state_hbm.1, f32[128,1024]{1,0:T(8,128)} %cotangent_hbm.1, f32[3,1024]{1,0:T(4,128)} %velocity_hbm.3, f32[1,1024]{1,0:T(1,128)} %bitcast.3, f32[128,1024]{1,0:T(8,128)} %retained_hbm.1, ...), custom_call_target="tpu_custom_call" | custom-call | tf_op jit(solution)/shard_map/exchange/pallas_call | solution.py:610
  35.1 6.8 %merge.1 = (f32[128,1024]{1,0:T(8,128)}, f32[128,1024]{1,0:T(8,128)}, f32[1,16]{1,0:T(1,128)}) custom-call(f32[128,1024]{1,0:T(8,128)S(1)} %get-tuple-element.10.part_advanced, f32[128,1024]{1,0:T(8,128)S(1)} %get-tuple-element.11.part_adjoint, f32[6,192,128]{2,1,0:T(8,128)S(1)} %get-tuple-element.12.arrived, f32[8,1,128]{2,1,0:T(1,128)S(1)} %get-tuple-element.13.sums, ...), custom_call_target="tpu_custom_call" | custom-call | tf_op jit(solution)/shard_map/merge/pallas_call | solution.py:667

commit v2 on v1

--- a/solution.py
+++ b/solution.py
@@ -19,6 +19,8 @@
 TABLE = FACES + ROUNDS * CAP + 8
 N_SUB = 8
 BLOCKS = 128
+UNROLL_BUILD = 1
+UNROLL_CLOSE = 8
 MESH = pl.DeviceIdType.MESH
 F32 = jnp.float32
 BF16 = jnp.bfloat16
@@ -149,11 +151,11 @@
     send_hbm,
     forward_hbm,
     backward_hbm,
-    expansion_hbm,
     advanced,
     adjoint,
     arrived_out,
     sums_out,
+    outer_rows,
     state,
     cotangent,
     velocity,
@@ -162,12 +164,10 @@
     block,
     forward_op,
     backward_op,
-    expansion,
     kappa_ref,
     source_index,
     send_index,
     table,
-    pairs,
     outgoing,
     kappa_rows,
     sums_row,
@@ -193,7 +193,6 @@
             ("dispersion", dispersion_hbm, dispersion),
             ("forward", forward_hbm, forward_op),
             ("backward", backward_hbm, backward_op),
-            ("expansion", expansion_hbm, expansion),
         ]
     ):
         loads[name] = pltpu.make_async_copy(src, dst, in_sem.at[number])
@@ -220,36 +219,40 @@
         )
 
     loads["velocity"].start()
-    loads["kappa"].start()
     for chunk in range(ELEMS // 128):
         for number in range(2):
             field_load(number, chunk).start()
-    for load in send_loads:
-        load.start()
-    for load in source_loads:
-        load.start()
-    for chunk in range(ELEMS // 128):
-        field_load(2, chunk).start()
-    for name in ("block", "dispersion", "forward", "backward", "expansion"):
-        loads[name].start()
 
     def dom_partner(offset):
-        return lax.rem(dom + (offset + n_dom), n_dom)
+        return dom + offset
+
+    def has_partner(offset):
+        return dom >= -offset if offset < 0 else dom < n_dom - offset
 
     def sub_partner(turn):
         return lax.rem(sub + turn, N_SUB)
 
     offsets = [n - REACH if n < REACH else n - REACH + 1 for n in range(ROUNDS)]
     barrier = pltpu.get_barrier_semaphore()
+    partner_count = N_SUB - 1
     for offset in offsets:
-        pl.semaphore_signal(
-            barrier, inc=1, device_id={"dom": dom_partner(offset)}, device_id_type=MESH
-        )
+        partner_count = partner_count + has_partner(offset).astype(jnp.int32)
+
+        @pl.when(has_partner(offset))
+        def _(offset=offset):
+            pl.semaphore_signal(
+                barrier, inc=1, device_id={"dom": dom_partner(offset)}, device_id_type=MESH
+            )
+
     for turn in range(1, N_SUB):
         pl.semaphore_signal(
             barrier, inc=1, device_id={"sub": sub_partner(turn)}, device_id_type=MESH
         )
 
+    for load in send_loads:
+        load.start()
+    loads["kappa"].start()
+
     zero_tile = jnp.zeros((8, 128), F32)
 
     def clear(step, carry):
@@ -257,13 +260,6 @@
         return carry
 
     lax.fori_loop(0, (TABLE - FACES) // 8, clear, 0, unroll=17)
-
-    lane_row = iota((1, 128), 1)
-    own_row = jnp.zeros((1, 128), F32)
-    loads["kappa"].wait()
-    for place in range(16):
-        own_row = jnp.where(lane_row == sub * 16 + place, kappa_ref[place], own_row)
-    kappa_rows[0] = own_row
 
     loads["velocity"].wait()
     low_lanes = iota((128, 128), 1) < 64
@@ -289,12 +285,20 @@
             )
         return carry
 
-    lax.fori_loop(0, ELEMS // 128, build, 0)
+    lax.fori_loop(0, ELEMS // 128, build, 0, unroll=UNROLL_BUILD)
     low_row = iota((1, 128), 1) < 64
 
     for load in send_loads:
         load.wait()
-    pl.semaphore_wait(barrier, ROUNDS + N_SUB - 1)
+    pl.semaphore_wait(barrier, partner_count)
+
+    group = 32
+    lane_row = iota((1, 128), 1)
+    own_row = jnp.zeros((1, 128), F32)
+    loads["kappa"].wait()
+    for place in range(16):
+        own_row = jnp.where(lane_row == sub * 16 + place, kappa_ref[place], own_row)
+    kappa_rows[0] = own_row
 
     kappa_copies = [
         pltpu.make_async_remote_copy(
@@ -307,12 +311,10 @@
         )
         for turn in range(1, N_SUB)
     ]
-    for copy in kappa_copies:
-        copy.start()
-
-    group = 32
+
     round_copies = []
-    for number in (0, 5, 1, 4, 2, 3):
+    round_order = (0, 5, 1, 4, 2, 3)
+    for turn, number in enumerate(round_order):
 
         def gather(step, carry, number=number):
             base = step * group
@@ -327,7 +329,6 @@
                 outgoing[number, pl.ds(base + place, 1), :] = values[place]
             return carry
 
-        lax.fori_loop(0, HALF // group, gather, 0)
         copy = pltpu.make_async_remote_copy(
             src_ref=outgoing.at[number],
             dst_ref=arrived_out.at[ROUNDS - 1 - number],
@@ -336,8 +337,86 @@
             device_id={"dom": dom_partner(offsets[number])},
             device_id_type=MESH,
         )
+
+        @pl.when(has_partner(offsets[number]))
+        def _(gather=gather, copy=copy):
+            lax.fori_loop(0, HALF // group, gather, 0)
+            copy.start()
+
+        round_copies.append(copy)
+        if turn == 1:
+            for copy in kappa_copies:
+                copy.start()
+            loads["block"].start()
+            for chunk in range(ELEMS // 128):
+                field_load(2, chunk).start()
+        if turn == 3:
+            for load in source_loads:
+                load.start()
+            for name in ("dispersion", "forward", "backward"):
+                loads[name].start()
+
+    width = 256
+    sublane = iota((8, width), 0)
+
+    def two_chunks(ref, chunk):
+        return jnp.concatenate([ref[2 * chunk], ref[2 * chunk + 1]], axis=1)
+
+    def free_sites(chunk):
+        gain = jnp.where(iota((128, width), 0) < 64, 1.0, SECOND_SPECIES)
+        return gain * (1.0 - two_chunks(retained, chunk))
+
+    def block_hits(cols):
+        return (iota((BLOCKS, width), 0) == block[:, cols]).astype(F32).astype(BF16)
+
+    loads["block"].wait()
+    for chunk in range(ELEMS // 128):
+        field_load(2, chunk).wait()
+    sums_acc[...] = jnp.zeros_like(sums_acc)
+
+    def block_sums(chunk, carry):
+        cols = pl.ds(pl.multiple_of(chunk * width, width), width)
+        product = free_sites(chunk) * two_chunks(cotangent, chunk) * two_chunks(state, chunk)
+        terms = jnp.sum(product, axis=0, keepdims=True)
+        term_parts = jnp.concatenate(
+            list(split3(terms)) + [jnp.zeros((13, width), BF16)], axis=0
+        )
+        sums_acc[...] += lax.dot_general(
+            term_parts, block_hits(cols), (((1,), (1,)), ((), ())), preferred_element_type=F32
+        )
+        return carry
+
+    lax.fori_loop(0, ELEMS // width, block_sums, 0)
+    sums_row[...] = (sums_acc[0:1] + sums_acc[1:2]) + sums_acc[2:3]
+
+    sums_out[0] = sums_row[...]
+    sums_copies = [
+        pltpu.make_async_remote_copy(
+            src_ref=sums_row,
+            dst_ref=sums_out.at[turn],
+            send_sem=sums_send.at[turn],
+            recv_sem=sums_recv.at[turn],
+            device_id={"sub": sub_partner(turn)},
+            device_id_type=MESH,
+        )
+        for turn in range(1, N_SUB)
+    ]
+    for copy in sums_copies:
         copy.start()
-        round_copies.append(copy)
+
+    for load in source_loads:
+        load.wait()
+
+    def pick(step, carry):
+        base = step * (2 * group)
+        values = [
+            table[pl.ds(source_index[base + place], 1), :] for place in range(2 * group)
+        ]
+        for place in range(2 * group):
+            outer_rows[pl.ds(base + place, 1), :] = values[place]
+        return carry
+
+    lax.fori_loop(0, FACES // (2 * group), pick, 0)
 
     for copy in kappa_copies:
         copy.wait_recv()
@@ -347,29 +426,19 @@
     slab_parts = jnp.concatenate(
         list(split3(slab)) + [jnp.zeros((13, 128), BF16)], axis=0
     )
-    for name in ("block", "dispersion", "forward", "backward"):
+    for name in ("dispersion", "forward", "backward"):
         loads[name].wait()
-    for chunk in range(ELEMS // 128):
-        field_load(2, chunk).wait()
-    sums_acc[...] = jnp.zeros_like(sums_acc)
-
-    width = 256
-    sublane = iota((8, width), 0)
 
     def volume(chunk, carry):
         start = pl.multiple_of(chunk * width, width)
         cols = pl.ds(start, width)
-        hits = (iota((BLOCKS, width), 0) == block[:, cols]).astype(F32).astype(BF16)
-        rates = jnp.dot(slab_parts, hits, preferred_element_type=F32)
+        rates = jnp.dot(slab_parts, block_hits(cols), preferred_element_type=F32)
         elem_rate = (rates[0:1] + rates[1:2]) + rates[2:3]
         speeds = velocity[:, cols]
         spread = dispersion[:, cols] * STEP
 
-        def two_chunks(ref):
-            return jnp.concatenate([ref[2 * chunk], ref[2 * chunk + 1]], axis=1)
-
-        field = two_chunks(state)
-        dual = two_chunks(cotangent)
+        field = two_chunks(state, chunk)
+        dual = two_chunks(cotangent, chunk)
         weights = [face_weight(speeds, face) for face in range(6)]
         along_i = jnp.where(
             sublane % 4 == 0, weights[0], jnp.where(sublane % 4 == 3, weights[1], 0.0)
@@ -382,16 +451,8 @@
         tiles += [by_j[0], by_j[1], by_j[0], by_j[1]]
         tiles += [by_j[0] + weights[5], by_j[1] + weights[5]]
         face_part = jnp.concatenate(tiles + tiles, axis=0)
-        gain = jnp.where(iota((128, width), 0) < 64, 1.0, SECOND_SPECIES)
-        free = gain * (1.0 - two_chunks(retained))
+        free = free_sites(chunk)
         factor = 1.0 + STEP * (face_part - elem_rate * free)
-        terms = jnp.sum(free * dual * field, axis=0, keepdims=True)
-        term_parts = jnp.concatenate(
-            list(split3(terms)) + [jnp.zeros((13, width), BF16)], axis=0
-        )
-        sums_acc[...] += lax.dot_general(
-            term_parts, hits, (((1,), (1,)), ((), ())), preferred_element_type=F32
-        )
         for values, operator, target in (
             (field, forward_op, advanced),
             (dual, backward_op, adjoint),
@@ -412,63 +473,13 @@
         return carry
 
     lax.fori_loop(0, ELEMS // width, volume, 0)
-    sums_row[...] = (sums_acc[0:1] + sums_acc[1:2]) + sums_acc[2:3]
-
-    sums_out[0] = sums_row[...]
-    sums_copies = [
-        pltpu.make_async_remote_copy(
-            src_ref=sums_row,
-            dst_ref=sums_out.at[turn],
-            send_sem=sums_send.at[turn],
-            recv_sem=sums_recv.at[turn],
-            device_id={"sub": sub_partner(turn)},
-            device_id_type=MESH,
-        )
-        for turn in range(1, N_SUB)
-    ]
-    for copy in sums_copies:
-        copy.start()
-
-    for load in source_loads:
-        load.wait()
-    for pair in range(3):
-
-        def pick(step, carry, pair=pair):
-            base = step * group
-            values = []
-            for place in range(group):
-                first = source_index[2 * pair * ELEMS + base + place]
-                second = source_index[(2 * pair + 1) * ELEMS + base + place]
-                values.append(
-                    jnp.where(low_row, table[pl.ds(first, 1), :], table[pl.ds(second, 1), :])
-                )
-            for place in range(group):
-                pairs[pl.ds(pair * ELEMS + base + place, 1), :] = values[place]
-            return carry
-
-        lax.fori_loop(0, ELEMS // group, pick, 0)
-
-    loads["expansion"].wait()
-
-    def close(chunk, carry):
-        start = pl.multiple_of(chunk * 128, 128)
-        cols = pl.ds(start, 128)
-        added = expand_faces(
-            lambda pair: pairs[pl.ds(pl.multiple_of(pair * ELEMS + start, 128), 128), :],
-            velocity[:, cols],
-            expansion[...],
-        )
-        advanced[:, cols] += added[0]
-        adjoint[:, cols] += added[1]
-        return carry
-
-    lax.fori_loop(0, ELEMS // 128, close, 0)
     for copy in kappa_copies:
         copy.wait_send()
     for copy in sums_copies:
         copy.wait()
-    for copy in round_copies:
-        copy.wait()
+    for number, copy in zip(round_order, round_copies):
+        pl.when(has_partner(offsets[number]))(copy.wait_send)
+        pl.when(has_partner(offsets[ROUNDS - 1 - number]))(copy.wait_recv)
 
 
 def merge_kernel(
@@ -476,23 +487,25 @@
     part_adjoint,
     arrived,
     sums,
+    outer_rows,
     velocity_hbm,
     send_hbm,
     expansion_hbm,
     advanced_out,
     adjoint_out,
     grad_out,
+    spread,
     advanced,
     adjoint,
     velocity,
     expansion,
     send_index,
     rows,
-    spread,
     in_sem,
     index_sem,
     out_sem,
 ):
+    del outer_rows
     sub = lax.axis_index("sub")
     loads = [
         pltpu.make_async_copy(src, dst, in_sem.at[number])
@@ -513,14 +526,6 @@
         load.start()
     for load in loads:
         load.start()
-    zero_tile = jnp.zeros((8, 128), F32)
-
-    def clear(step, carry):
-        for place in range(16):
-            spread[pl.ds(pl.multiple_of(step * 128 + place * 8, 8), 8), :] = zero_tile
-        return carry
-
-    lax.fori_loop(0, FACES // 128, clear, 0)
     low_lanes = iota((HALF, 128), 1) < 64
     for number in range(ROUNDS):
         values = arrived[number]
@@ -575,7 +580,7 @@
             copy.start()
         return carry
 
-    lax.fori_loop(0, ELEMS // 128, close, 0)
+    lax.fori_loop(0, ELEMS // 128, close, 0, unroll=UNROLL_CLOSE)
 
     def finish(chunk, carry):
         for copy in results(chunk):
@@ -607,16 +612,17 @@
         face_source, send_face, kappa = map(kept, (face_source, send_face, kappa))
         dispersion = kept(dispersion.reshape(1, ELEMS))
         elem_block = kept(elem_block.reshape(1, ELEMS))
-        part_advanced, part_adjoint, arrived, sums = pl.pallas_call(
+        part_advanced, part_adjoint, arrived, sums, outer_rows = pl.pallas_call(
             functools.partial(exchange_kernel, n_dom),
             out_shape=(
                 field,
                 field,
                 jax.ShapeDtypeStruct((ROUNDS, HALF, 128), F32),
                 jax.ShapeDtypeStruct((N_SUB, 1, 128), F32),
+                jax.ShapeDtypeStruct((FACES + 8, 128), F32),
             ),
-            in_specs=[in_hbm] * 12,
-            out_specs=(in_vmem,) * 4,
+            in_specs=[in_hbm] * 11,
+            out_specs=(in_vmem,) * 5,
             scratch_shapes=[
                 pltpu.VMEM((ELEMS // 128, 128, 128), F32),
                 pltpu.VMEM((ELEMS // 128, 128, 128), F32),
@@ -626,12 +632,10 @@
                 pltpu.VMEM((1, ELEMS), jnp.int32),
                 pltpu.VMEM((512, 384), BF16),
                 pltpu.VMEM((512, 384), BF16),
-                pltpu.VMEM((128, 384), BF16),
                 pltpu.SMEM((16,), F32),
                 pltpu.SMEM((FACES,), jnp.int32),
                 pltpu.SMEM((ROUNDS * CAP,), jnp.int32),
                 pltpu.VMEM((TABLE, 128), F32),
-                pltpu.VMEM((3 * ELEMS, 128), F32),
                 pltpu.VMEM((ROUNDS, HALF, 128), F32),
                 pltpu.VMEM((N_SUB, 1, 128), F32),
                 pltpu.VMEM((1, 128), F32),
@@ -662,13 +666,18 @@
             send_face,
             forward_op,
             backward_op,
-            expansion,
-        )
-        advanced, adjoint, grad = pl.pallas_call(
+        )
+        advanced, adjoint, grad, _ = pl.pallas_call(
             merge_kernel,
-            out_shape=(field, field, jax.ShapeDtypeStruct((1, 16), F32)),
-            in_specs=[in_vmem] * 4 + [in_hbm] * 3,
-            out_specs=(in_hbm, in_hbm, in_vmem),
+            out_shape=(
+                field,
+                field,
+                jax.ShapeDtypeStruct((1, 16), F32),
+                jax.ShapeDtypeStruct((FACES + 8, 128), F32),
+            ),
+            in_specs=[in_vmem] * 5 + [in_hbm] * 3,
+            out_specs=(in_hbm, in_hbm, in_vmem, in_vmem),
+            input_output_aliases={4: 3},
             scratch_shapes=[
                 pltpu.VMEM((128, ELEMS), F32),
                 pltpu.VMEM((128, ELEMS), F32),
@@ -676,14 +685,13 @@
                 pltpu.VMEM((128, 384), BF16),
                 pltpu.SMEM((ROUNDS * CAP,), jnp.int32),
                 pltpu.VMEM((ROUNDS * CAP, 128), F32),
-                pltpu.VMEM((FACES + 8, 128), F32),
                 dma((2,)),
                 dma((ROUNDS,)),
                 dma((2, ELEMS // 128)),
             ],
             compiler_params=pltpu.CompilerParams(vmem_limit_bytes=40 << 20),
             name="merge",
-        )(part_advanced, part_adjoint, arrived, sums, velocity, send_face, expansion)
+        )(part_advanced, part_adjoint, arrived, sums, outer_rows, velocity, send_face, expansion)
         return advanced, adjoint, grad.reshape(16)
 
     wide = P(None, ("dom", "sub"))

time: 42.1 us -> 32.6 us (0.77)
  the two profiles are of different devices: /device:TPU:1 before, /device:TPU:567 now
where the time goes in v2:
time: 32.6 us; the launch traced here: 32.3 us
  Pallas kernels  31.7 us (97%)
  between operations  0.64 us (2%)
    pallas_call x1, Pallas kernels, shards(): pl.pallas_call(functools.partial(exchange_kernel, n_dom), out_shape=(fiel...  26.4 us
    pallas_call x1, Pallas kernels, shards(): pl.pallas_call(merge_kernel, out_shape=(field, field, jax.ShapeDtypeStruc...  5.3 us

profile of v2, /device:TPU:567, one launch (start us, length us, event | category | flops | bytes accessed | tf_op | source)
XLA Modules:
  0.0 32.3 jit_solution(9078327857406392787)
XLA Ops:
  0.6 26.4 %exchange.1 = (f32[128,1024]{1,0:T(8,128)S(1)}, f32[128,1024]{1,0:T(8,128)S(1)}, f32[6,192,128]{2,1,0:T(8,128)S(1)}, f32[8,1,128]{2,1,0:T(1,128)S(1)}, f32[6152,128]{1,0:T(8,128)S(1)}) custom-call(f32[128,1024]{1,0:T(8,128)} %state_hbm.1, f32[128,1024]{1,0:T(8,128)} %cotangent_hbm.1, f32[3,1024]{1,0:T(4,128)} %velocity_hbm.3, f32[1,1024]{1,0:T(1,128)} %bitcast.3, ...), custom_call_target="tpu_custom_call" | custom-call | tf_op jit(solution)/shard_map/exchange/pallas_call | solution.py:615
  27.0 5.3 %merge.1 = (f32[128,1024]{1,0:T(8,128)}, f32[128,1024]{1,0:T(8,128)}, f32[1,16]{1,0:T(1,128)}, f32[6152,128]{1,0:T(8,128)S(1)}) custom-call(f32[128,1024]{1,0:T(8,128)S(1)} %get-tuple-element.11.part_advanced, f32[128,1024]{1,0:T(8,128)S(1)} %get-tuple-element.12.part_adjoint, ...), custom_call_target="tpu_custom_call", output_to_operand_aliasing={{3}: (4, {})} | custom-call | tf_op jit(solution)/shard_map/merge/pallas_call | solution.py:670

commit v3 on v2

--- a/solution.py
+++ b/solution.py
@@ -16,6 +16,7 @@
 FACES = 6 * ELEMS
 CAP = 384
 HALF = CAP // 2
+QUARTER = CAP // 4
 TABLE = FACES + ROUNDS * CAP + 8
 N_SUB = 8
 BLOCKS = 128
@@ -151,14 +152,17 @@
     send_hbm,
     forward_hbm,
     backward_hbm,
+    expansion_hbm,
     advanced,
     adjoint,
     arrived_out,
     sums_out,
     outer_rows,
+    velocity,
+    send_rows,
+    expansion,
     state,
     cotangent,
-    velocity,
     dispersion,
     retained,
     block,
@@ -193,6 +197,8 @@
             ("dispersion", dispersion_hbm, dispersion),
             ("forward", forward_hbm, forward_op),
             ("backward", backward_hbm, backward_op),
+            ("rows", send_hbm, send_rows),
+            ("expansion", expansion_hbm, expansion),
         ]
     ):
         loads[name] = pltpu.make_async_copy(src, dst, in_sem.at[number])
@@ -219,9 +225,8 @@
         )
 
     loads["velocity"].start()
-    for chunk in range(ELEMS // 128):
-        for number in range(2):
-            field_load(number, chunk).start()
+    for number in range(2):
+        field_load(number, 0).start()
 
     def dom_partner(offset):
         return dom + offset
@@ -249,6 +254,9 @@
             barrier, inc=1, device_id={"sub": sub_partner(turn)}, device_id_type=MESH
         )
 
+    for chunk in range(1, ELEMS // 128):
+        for number in range(2):
+            field_load(number, chunk).start()
     for load in send_loads:
         load.start()
     loads["kappa"].start()
@@ -262,26 +270,19 @@
     lax.fori_loop(0, (TABLE - FACES) // 8, clear, 0, unroll=17)
 
     loads["velocity"].wait()
-    low_lanes = iota((128, 128), 1) < 64
-
     def build(chunk, carry):
         field_load(0, chunk).wait()
         field_load(1, chunk).wait()
         start = pl.multiple_of(chunk * 128, 128)
         cols = pl.ds(start, 128)
         speeds = velocity[:, cols]
-        for pair in range(3):
-            parts = []
-            for face in (2 * pair, 2 * pair + 1):
-                parts.append(trace_of(state, face, chunk))
-                parts.append(trace_of(cotangent, face, chunk) * (-face_weight(speeds, face)))
-            rows = jnp.transpose(jnp.concatenate(parts, axis=0))
-            turned = pltpu.roll(rows, 64, 1)
-            table[pl.ds(pl.multiple_of(2 * pair * ELEMS + start, 128), 128), :] = jnp.where(
-                low_lanes, rows, turned
-            )
-            table[pl.ds(pl.multiple_of((2 * pair + 1) * ELEMS + start, 128), 128), :] = jnp.where(
-                low_lanes, turned, rows
+        for face in range(6):
+            both = [
+                trace_of(state, face, chunk),
+                trace_of(cotangent, face, chunk) * (-face_weight(speeds, face)),
+            ]
+            table[pl.ds(pl.multiple_of(face * ELEMS + start, 128), 128), :] = jnp.transpose(
+                jnp.concatenate(both + both, axis=0)
             )
         return carry
 
@@ -290,7 +291,6 @@
 
     for load in send_loads:
         load.wait()
-    pl.semaphore_wait(barrier, partner_count)
 
     group = 32
     lane_row = iota((1, 128), 1)
@@ -313,8 +313,9 @@
     ]
 
     round_copies = []
-    round_order = (0, 5, 1, 4, 2, 3)
-    for turn, number in enumerate(round_order):
+    round_order = [(r, half) for r in ((0, 5), (1, 4), (2, 3)) for half in range(2)]
+    round_order = [(number, half) for pair, half in round_order for number in pair]
+    for turn, (number, half) in enumerate(round_order):
 
         def gather(step, carry, number=number):
             base = step * group
@@ -329,31 +330,33 @@
                 outgoing[number, pl.ds(base + place, 1), :] = values[place]
             return carry
 
+        part = pl.ds(half * QUARTER, QUARTER)
         copy = pltpu.make_async_remote_copy(
-            src_ref=outgoing.at[number],
-            dst_ref=arrived_out.at[ROUNDS - 1 - number],
-            send_sem=send_sem.at[number],
-            recv_sem=recv_sem.at[ROUNDS - 1 - number],
+            src_ref=outgoing.at[number, part],
+            dst_ref=arrived_out.at[ROUNDS - 1 - number, part],
+            send_sem=send_sem.at[number, half],
+            recv_sem=recv_sem.at[ROUNDS - 1 - number, half],
             device_id={"dom": dom_partner(offsets[number])},
             device_id_type=MESH,
         )
 
-        @pl.when(has_partner(offsets[number]))
-        def _(gather=gather, copy=copy):
-            lax.fori_loop(0, HALF // group, gather, 0)
-            copy.start()
+        steps = QUARTER // group
+        lax.fori_loop(half * steps, (half + 1) * steps, gather, 0)
+        if turn == 0:
+            pl.semaphore_wait(barrier, partner_count)
+        pl.when(has_partner(offsets[number]))(copy.start)
 
         round_copies.append(copy)
-        if turn == 1:
+        if turn == 3:
             for copy in kappa_copies:
                 copy.start()
             loads["block"].start()
             for chunk in range(ELEMS // 128):
                 field_load(2, chunk).start()
-        if turn == 3:
+        if turn == 7:
             for load in source_loads:
                 load.start()
-            for name in ("dispersion", "forward", "backward"):
+            for name in ("dispersion", "forward", "backward", "rows", "expansion"):
                 loads[name].start()
 
     width = 256
@@ -426,7 +429,7 @@
     slab_parts = jnp.concatenate(
         list(split3(slab)) + [jnp.zeros((13, 128), BF16)], axis=0
     )
-    for name in ("dispersion", "forward", "backward"):
+    for name in ("dispersion", "forward", "backward", "rows", "expansion"):
         loads[name].wait()
 
     def volume(chunk, carry):
@@ -477,7 +480,7 @@
         copy.wait_send()
     for copy in sums_copies:
         copy.wait()
-    for number, copy in zip(round_order, round_copies):
+    for (number, _), copy in zip(round_order, round_copies):
         pl.when(has_partner(offsets[number]))(copy.wait_send)
         pl.when(has_partner(offsets[ROUNDS - 1 - number]))(copy.wait_recv)
 
@@ -488,43 +491,29 @@
     arrived,
     sums,
     outer_rows,
-    velocity_hbm,
-    send_hbm,
-    expansion_hbm,
+    velocity,
+    send_rows,
+    expansion,
     advanced_out,
     adjoint_out,
     grad_out,
     spread,
     advanced,
     adjoint,
-    velocity,
-    expansion,
     send_index,
     rows,
-    in_sem,
     index_sem,
     out_sem,
 ):
     del outer_rows
     sub = lax.axis_index("sub")
-    loads = [
-        pltpu.make_async_copy(src, dst, in_sem.at[number])
-        for number, (src, dst) in enumerate(
-            [
-                (velocity_hbm, velocity),
-                (expansion_hbm, expansion),
-            ]
-        )
-    ]
     index_loads = [
         pltpu.make_async_copy(
-            send_hbm.at[number], send_index.at[pl.ds(number * CAP, CAP)], index_sem.at[number]
+            send_rows.at[number], send_index.at[pl.ds(number * CAP, CAP)], index_sem.at[number]
         )
         for number in range(ROUNDS)
     ]
     for load in index_loads:
-        load.start()
-    for load in loads:
         load.start()
     low_lanes = iota((HALF, 128), 1) < 64
     for number in range(ROUNDS):
@@ -534,7 +523,7 @@
         rows[pl.ds(number * CAP + HALF, HALF), :] = jnp.where(low_lanes, turned, values)
     for load in index_loads:
         load.wait()
-    group = 64
+    group = 384
 
     def scatter(step, carry):
         base = step * group
@@ -544,8 +533,6 @@
         return carry
 
     lax.fori_loop(0, ROUNDS * CAP // group, scatter, 0)
-    for load in loads:
-        load.wait()
     total = jnp.zeros((1, 128), F32)
     for turn in range(N_SUB):
         total = total + sums[turn]
@@ -612,7 +599,7 @@
         face_source, send_face, kappa = map(kept, (face_source, send_face, kappa))
         dispersion = kept(dispersion.reshape(1, ELEMS))
         elem_block = kept(elem_block.reshape(1, ELEMS))
-        part_advanced, part_adjoint, arrived, sums, outer_rows = pl.pallas_call(
+        handed_on = pl.pallas_call(
             functools.partial(exchange_kernel, n_dom),
             out_shape=(
                 field,
@@ -620,13 +607,15 @@
                 jax.ShapeDtypeStruct((ROUNDS, HALF, 128), F32),
                 jax.ShapeDtypeStruct((N_SUB, 1, 128), F32),
                 jax.ShapeDtypeStruct((FACES + 8, 128), F32),
+                jax.ShapeDtypeStruct((3, ELEMS), F32),
+                jax.ShapeDtypeStruct((ROUNDS, CAP), jnp.int32),
+                jax.ShapeDtypeStruct((128, 384), BF16),
             ),
-            in_specs=[in_hbm] * 11,
-            out_specs=(in_vmem,) * 5,
+            in_specs=[in_hbm] * 12,
+            out_specs=(in_vmem,) * 8,
             scratch_shapes=[
                 pltpu.VMEM((ELEMS // 128, 128, 128), F32),
                 pltpu.VMEM((ELEMS // 128, 128, 128), F32),
-                pltpu.VMEM((3, ELEMS), F32),
                 pltpu.VMEM((1, ELEMS), F32),
                 pltpu.VMEM((ELEMS // 128, 128, 128), F32),
                 pltpu.VMEM((1, ELEMS), jnp.int32),
@@ -640,11 +629,11 @@
                 pltpu.VMEM((N_SUB, 1, 128), F32),
                 pltpu.VMEM((1, 128), F32),
                 pltpu.VMEM((16, 128), F32),
-                dma((7,)),
+                dma((9,)),
                 dma((3, ELEMS // 128)),
                 dma((ROUNDS + 6,)),
-                dma((ROUNDS,)),
-                dma((ROUNDS,)),
+                dma((ROUNDS, 2)),
+                dma((ROUNDS, 2)),
                 dma((N_SUB,)),
                 dma((N_SUB,)),
                 dma((N_SUB,)),
@@ -666,6 +655,7 @@
             send_face,
             forward_op,
             backward_op,
+            expansion,
         )
         advanced, adjoint, grad, _ = pl.pallas_call(
             merge_kernel,
@@ -675,23 +665,20 @@
                 jax.ShapeDtypeStruct((1, 16), F32),
                 jax.ShapeDtypeStruct((FACES + 8, 128), F32),
             ),
-            in_specs=[in_vmem] * 5 + [in_hbm] * 3,
+            in_specs=[in_vmem] * 8,
             out_specs=(in_hbm, in_hbm, in_vmem, in_vmem),
             input_output_aliases={4: 3},
             scratch_shapes=[
                 pltpu.VMEM((128, ELEMS), F32),
                 pltpu.VMEM((128, ELEMS), F32),
-                pltpu.VMEM((3, ELEMS), F32),
-                pltpu.VMEM((128, 384), BF16),
                 pltpu.SMEM((ROUNDS * CAP,), jnp.int32),
                 pltpu.VMEM((ROUNDS * CAP, 128), F32),
-                dma((2,)),
                 dma((ROUNDS,)),
                 dma((2, ELEMS // 128)),
             ],
             compiler_params=pltpu.CompilerParams(vmem_limit_bytes=40 << 20),
             name="merge",
-        )(part_advanced, part_adjoint, arrived, sums, outer_rows, velocity, send_face, expansion)
+        )(*handed_on)
         return advanced, adjoint, grad.reshape(16)
 
     wide = P(None, ("dom", "sub"))

time: 32.6 us -> 31.6 us (0.969)
  the two profiles are of different devices: /device:TPU:567 before, /device:TPU:561 now
where the time goes in v3:
time: 31.6 us; the launch traced here: 31.4 us
  Pallas kernels  30.8 us (97%)
  between operations  0.64 us (2%)
    pallas_call x1, Pallas kernels, shards(): pl.pallas_call(functools.partial(exchange_kernel, n_dom), out_shape=(fiel...  25.9 us
    pallas_call x1, Pallas kernels, shards(): pl.pallas_call(merge_kernel, out_shape=(field, field, jax.ShapeDtypeStruc...  4.9 us

profile of v3, /device:TPU:561, one launch (start us, length us, event | category | flops | bytes accessed | tf_op | source)
XLA Modules:
  0.0 31.4 jit_solution(11797794585040110746)
XLA Ops:
  0.6 25.9 %exchange.1 = (f32[128,1024]{1,0:T(8,128)S(1)}, f32[128,1024]{1,0:T(8,128)S(1)}, f32[6,192,128]{2,1,0:T(8,128)S(1)}, f32[8,1,128]{2,1,0:T(1,128)S(1)}, f32[6152,...) custom-call(f32[128,1024]{1,0:T(8,128)} %state_hbm.1, ...), custom_call_target="tpu_custom_call" | custom-call | tf_op jit(solution)/shard_map/exchange/pallas_call | solution.py:602
  26.5 4.9 %merge.1 = (f32[128,1024]{1,0:T(8,128)}, f32[128,1024]{1,0:T(8,128)}, f32[1,16]{1,0:T(1,128)}, f32[6152,128]{1,0:T(8,128)S(1)}) custom-call(f32[128,1024]{1,0:T(8,128)S(1)} %get-tuple-element.14.part_advanced, f32[128,1024]{1,0:T(8,128)S(1)} %get-tuple-element.15.part_adjoint, ...), custom_call_target="tpu_custom_call", output_to_operand_aliasing={{3}: (4, {})} | custom-call | tf_op jit(solution)/shard_map/merge/pallas_call | solution.py:660

commit v4 on v3

--- a/solution.py
+++ b/solution.py
@@ -20,7 +20,6 @@
 TABLE = FACES + ROUNDS * CAP + 8
 N_SUB = 8
 BLOCKS = 128
-UNROLL_BUILD = 1
 UNROLL_CLOSE = 8
 MESH = pl.DeviceIdType.MESH
 F32 = jnp.float32
@@ -286,7 +285,7 @@
             )
         return carry
 
-    lax.fori_loop(0, ELEMS // 128, build, 0, unroll=UNROLL_BUILD)
+    lax.fori_loop(0, ELEMS // 128, build, 0)
     low_row = iota((1, 128), 1) < 64
 
     for load in send_loads:
@@ -313,7 +312,7 @@
     ]
 
     round_copies = []
-    round_order = [(r, half) for r in ((0, 5), (1, 4), (2, 3)) for half in range(2)]
+    round_order = [(r, half) for r in ((0, 5), (2, 3), (1, 4)) for half in range(2)]
     round_order = [(number, half) for pair, half in round_order for number in pair]
     for turn, (number, half) in enumerate(round_order):
 
@@ -406,20 +405,6 @@
     ]
     for copy in sums_copies:
         copy.start()
-
-    for load in source_loads:
-        load.wait()
-
-    def pick(step, carry):
-        base = step * (2 * group)
-        values = [
-            table[pl.ds(source_index[base + place], 1), :] for place in range(2 * group)
-        ]
-        for place in range(2 * group):
-            outer_rows[pl.ds(base + place, 1), :] = values[place]
-        return carry
-
-    lax.fori_loop(0, FACES // (2 * group), pick, 0)
 
     for copy in kappa_copies:
         copy.wait_recv()
@@ -476,6 +461,20 @@
         return carry
 
     lax.fori_loop(0, ELEMS // width, volume, 0)
+    for load in source_loads:
+        load.wait()
+
+    def pick(step, carry):
+        base = step * (2 * group)
+        values = [
+            table[pl.ds(source_index[base + place], 1), :] for place in range(2 * group)
+        ]
+        for place in range(2 * group):
+            outer_rows[pl.ds(base + place, 1), :] = values[place]
+        return carry
+
+    lax.fori_loop(0, FACES // (2 * group), pick, 0)
+
     for copy in kappa_copies:
         copy.wait_send()
     for copy in sums_copies:
@@ -524,15 +523,16 @@
     for load in index_loads:
         load.wait()
     group = 384
-
-    def scatter(step, carry):
-        base = step * group
-        values = [rows[pl.ds(base + place, 1), :] for place in range(group)]
-        for place in range(group):
-            spread[pl.ds(send_index[base + place], 1), :] = values[place]
-        return carry
-
-    lax.fori_loop(0, ROUNDS * CAP // group, scatter, 0)
+    for number in range(ROUNDS):
+
+        def scatter(step, carry, number=number):
+            base = number * CAP + step * group
+            values = [rows[pl.ds(base + place, 1), :] for place in range(group)]
+            for place in range(group):
+                spread[pl.ds(send_index[base + place], 1), :] = values[place]
+            return carry
+
+        lax.fori_loop(0, CAP // group, scatter, 0)
     total = jnp.zeros((1, 128), F32)
     for turn in range(N_SUB):
         total = total + sums[turn]

time: 31.6 us -> 29.4 us (0.930)
  the two profiles are of different devices: /device:TPU:561 before, /device:TPU:1 now
where the time goes in v4:
time: 29.4 us; the launch traced here: 29.2 us
  Pallas kernels  28.6 us (97%)
  between operations  0.64 us (2%)
    pallas_call x1, Pallas kernels, shards(): pl.pallas_call(functools.partial(exchange_kernel, n_dom), out_shape=(fiel...  24.3 us
    pallas_call x1, Pallas kernels, shards(): pl.pallas_call(merge_kernel, out_shape=(field, field, jax.ShapeDtypeStruc...  4.27 us

profile of v4, /device:TPU:1, one launch (start us, length us, event | category | flops | bytes accessed | tf_op | source)
XLA Modules:
  0.0 29.2 jit_solution(6235895606390539973)
XLA Ops:
  0.6 24.3 %exchange.1 = (f32[128,1024]{1,0:T(8,128)S(1)}, f32[128,1024]{1,0:T(8,128)S(1)}, f32[6,192,128]{2,1,0:T(8,128)S(1)}, f32[8,1,128]{2,1,0:T(1,128)S(1)}, f32[6152,...) custom-call(f32[128,1024]{1,0:T(8,128)} %state_hbm.1, ...), custom_call_target="tpu_custom_call" | custom-call | tf_op jit(solution)/shard_map/exchange/pallas_call | solution.py:602
  24.9 4.3 %merge.1 = (f32[128,1024]{1,0:T(8,128)}, f32[128,1024]{1,0:T(8,128)}, f32[1,16]{1,0:T(1,128)}, f32[6152,128]{1,0:T(8,128)S(1)}) custom-call(f32[128,1024]{1,0:T(8,128)S(1)} %get-tuple-element.14.part_advanced, f32[128,1024]{1,0:T(8,128)S(1)} %get-tuple-element.15.part_adjoint, ...), custom_call_target="tpu_custom_call", output_to_operand_aliasing={{3}: (4, {})} | custom-call | tf_op jit(solution)/shard_map/merge/pallas_call | solution.py:660

commit v5 on v4

--- a/solution.py
+++ b/solution.py
@@ -312,8 +312,8 @@
     ]
 
     round_copies = []
-    round_order = [(r, half) for r in ((0, 5), (2, 3), (1, 4)) for half in range(2)]
-    round_order = [(number, half) for pair, half in round_order for number in pair]
+    round_order = [(0, 0), (5, 0), (2, 0), (3, 0), (0, 1), (5, 1), (2, 1), (3, 1)]
+    round_order += [(1, 0), (4, 0), (1, 1), (4, 1)]
     for turn, (number, half) in enumerate(round_order):
 
         def gather(step, carry, number=number):

time: 29.4 us -> 29.8 us (1.014)
  no operation moved by 1% of the time
where the time goes in v5:
time: 29.8 us; the launch traced here: 29.4 us
  Pallas kernels  28.7 us (96%)
  between operations  0.64 us (2%)
    pallas_call x1, Pallas kernels, shards(): pl.pallas_call(functools.partial(exchange_kernel, n_dom), out_shape=(fiel...  24.5 us
    pallas_call x1, Pallas kernels, shards(): pl.pallas_call(merge_kernel, out_shape=(field, field, jax.ShapeDtypeStruc...  4.27 us

profile of v5, /device:TPU:1, one launch (start us, length us, event | category | flops | bytes accessed | tf_op | source)
XLA Modules:
  0.0 29.4 jit_solution(6261315641907897211)
XLA Ops:
  0.6 24.5 %exchange.1 = (f32[128,1024]{1,0:T(8,128)S(1)}, f32[128,1024]{1,0:T(8,128)S(1)}, f32[6,192,128]{2,1,0:T(8,128)S(1)}, f32[8,1,128]{2,1,0:T(1,128)S(1)}, f32[6152,...) custom-call(f32[128,1024]{1,0:T(8,128)} %state_hbm.1, ...), custom_call_target="tpu_custom_call" | custom-call | tf_op jit(solution)/shard_map/exchange/pallas_call | solution.py:602
  25.1 4.3 %merge.1 = (f32[128,1024]{1,0:T(8,128)}, f32[128,1024]{1,0:T(8,128)}, f32[1,16]{1,0:T(1,128)}, f32[6152,128]{1,0:T(8,128)S(1)}) custom-call(f32[128,1024]{1,0:T(8,128)S(1)} %get-tuple-element.14.part_advanced, f32[128,1024]{1,0:T(8,128)S(1)} %get-tuple-element.15.part_adjoint, ...), custom_call_target="tpu_custom_call", output_to_operand_aliasing={{3}: (4, {})} | custom-call | tf_op jit(solution)/shard_map/merge/pallas_call | solution.py:660
